TPU v7x, 32 devices: a whole 2x2x4 slice. The times are simulated.
32 devices in a mesh: dp: 8 (over z, x), tensor: 4 (over y, core).
Axes of the slice: x: 2, y: 2, z: 4, core: 2. Of those that a mesh axis runs over, the one named last changes fastest.
Arguments:
- hidden_in: bfloat16 [16384, 1024], P(('dp', 'tensor')), may hold values from -6 to 6
- norm_gain: float32 [2, 1024], replicated, may hold values from 0.5 to 1.5
- norm_shift: float32 [2, 1024], replicated, may hold values from -2 to 2
- qkv_weight: bfloat16 [3, 1024, 1024], P(None, 'dp', 'tensor'), may hold values from -0.1875 to 0.1875
- qv_bias: float32 [2, 1024], P(None, 'tensor'), may hold values from -2 to 2
- out_weight: bfloat16 [1024, 1024], P('tensor', 'dp'), may hold values from -0.75 to 0.75
- out_bias: float32 [2, 1024], replicated, may hold values from -2 to 2
- up_weight: bfloat16 [1024, 4096], P('dp', 'tensor'), may hold values from -0.1875 to 0.1875
- up_bias: float32 [4096], P('tensor'), may hold values from -2 to 2
- down_weight: bfloat16 [4096, 1024], P('tensor', 'dp'), may hold values from -0.09375 to 0.09375
- cotangent: bfloat16 [16384, 1024], P(('dp', 'tensor')), may hold values from -6 to 6
Outputs:
- block_out: float32 [16384, 1024], P(('dp', 'tensor'))
- grad_in: float32 [16384, 1024], P(('dp', 'tensor'))
- grad_norm_gain: float32 [2, 1024], replicated
- grad_norm_shift: float32 [2, 1024], replicated
- grad_qkv: float32 [3, 1024, 1024], P(None, 'dp', 'tensor')
- grad_qv_bias: float32 [2, 1024], P(None, 'tensor')
- grad_out_weight: float32 [1024, 1024], P('tensor', 'dp')
- grad_out_bias: float32 [2, 1024], replicated
- grad_up_weight: float32 [1024, 4096], P('dp', 'tensor')
- grad_up_bias: float32 [4096], P('tensor')
- grad_down_weight: float32 [4096, 1024], P('tensor', 'dp')
All inputs are finite; a program needn't handle non-finite values.
Results may differ from a plain program's by a relative error of at most 0.014.
Values may be sent and summed in bfloat16 or wider, within the bound.
No kernel may reach another device: no remote copies, remote signals or barrier semaphores. Data moves between devices by JAX's collectives and lax.ppermute only.
A program may use at most 192 MiB of HBM per device.

v0:
```python
import math

import jax
import jax.numpy as jnp
from jax import lax
from jax.sharding import PartitionSpec as P

HEADS = 16


def layer_norm(values, norm_gain, norm_shift):
    average = jnp.mean(values, axis=-1, keepdims=True)
    centered = values - average
    inverse = lax.rsqrt(jnp.mean(centered * centered, axis=-1, keepdims=True) + 1e-05)
    scaled = centered * inverse
    return (scaled * norm_gain + norm_shift, scaled, inverse)


def norm_backward(gradient, scaled, inverse, norm_gain):
    grad_scaled = gradient * norm_gain
    grad_mean = jnp.mean(grad_scaled, axis=-1, keepdims=True)
    grad_proj = jnp.mean(grad_scaled * scaled, axis=-1, keepdims=True)
    grad_input = inverse * (grad_scaled - grad_mean - scaled * grad_proj)
    return (grad_input, jnp.sum(gradient * scaled, axis=0), jnp.sum(gradient, axis=0))


def gelu_tanh(values):
    tanh_input = 0.7978845608 * (values + 0.044715 * values * values * values)
    return 0.5 * values * (1.0 + jnp.tanh(tanh_input))


def gelu_slope(values):
    tanh_input = 0.7978845608 * (values + 0.044715 * values * values * values)
    tangent = jnp.tanh(tanh_input)
    return 0.5 * (1.0 + tangent) + 0.5 * values * (1.0 - tangent * tangent) * 0.7978845608 * (
        1.0 + 3.0 * 0.044715 * values * values
    )


def block_scores(query_block, key_rows, slopes, offset):
    block_rows = query_block.shape[0]
    key_count = key_rows.shape[0]
    raw_scores = jnp.einsum(
        "qhd,khd->hqk", query_block, key_rows, preferred_element_type=jnp.float32
    )
    query_pos = offset + lax.broadcasted_iota(jnp.int32, (block_rows, key_count), 0)
    key_pos = lax.broadcasted_iota(jnp.int32, (block_rows, key_count), 1)
    distance = query_pos - key_pos
    scores = (
        raw_scores * (1.0 / math.sqrt(query_block.shape[2]))
        - slopes[:, None, None] * distance.astype(jnp.float32)[None]
    )
    return jnp.where((distance >= 0)[None], scores, -1000000000.0)


def attend_forward(queries, key_rows, value_rows, slopes, block_rows):
    length = key_rows.shape[0]

    def one_block(block_index):
        offset = block_index * block_rows
        query_block = lax.dynamic_slice_in_dim(queries, offset, block_rows, 0)
        masked = block_scores(query_block, key_rows, slopes, offset)
        maxima = jnp.max(masked, axis=-1, keepdims=True)
        weights = jnp.exp(masked - maxima)
        totals = jnp.sum(weights, axis=-1, keepdims=True)
        attention = (weights / totals).astype(jnp.bfloat16)
        mixed_block = jnp.einsum(
            "hqk,khd->qhd", attention, value_rows, preferred_element_type=jnp.float32
        )
        return (mixed_block.reshape(block_rows, -1), (maxima + jnp.log(totals))[:, :, 0])

    mixed_blocks, logsums = lax.map(one_block, jnp.arange(length // block_rows, dtype=jnp.int32))
    return (mixed_blocks.reshape(length, -1), logsums)


def attend_backward(queries, key_rows, value_rows, grad_mixed, logsums, slopes, block_rows):
    length = key_rows.shape[0]
    scale = 1.0 / math.sqrt(queries.shape[2])

    def one_block(carry, block_index):
        key_grad, value_grad = carry
        offset = block_index * block_rows
        query_block = lax.dynamic_slice_in_dim(queries, offset, block_rows, 0)
        grad_block = lax.dynamic_slice_in_dim(grad_mixed, offset, block_rows, 0)
        masked = block_scores(query_block, key_rows, slopes, offset)
        attention = jnp.exp(masked - logsums[block_index][:, :, None])
        grad_attention = jnp.einsum(
            "qhd,khd->hqk", grad_block, value_rows, preferred_element_type=jnp.float32
        )
        centering = jnp.sum(attention * grad_attention, axis=-1, keepdims=True)
        grad_scores = (attention * (grad_attention - centering)).astype(jnp.bfloat16)
        query_grad = (
            jnp.einsum("hqk,khd->qhd", grad_scores, key_rows, preferred_element_type=jnp.float32)
            * scale
        )
        key_grad = (
            key_grad
            + jnp.einsum(
                "hqk,qhd->khd", grad_scores, query_block, preferred_element_type=jnp.float32
            )
            * scale
        )
        value_grad = value_grad + jnp.einsum(
            "hqk,qhd->khd",
            attention.astype(jnp.bfloat16),
            grad_block,
            preferred_element_type=jnp.float32,
        )
        return ((key_grad, value_grad), query_grad)

    zero_rows = jnp.zeros(key_rows.shape, jnp.float32)
    (key_grad, value_grad), query_grad = lax.scan(
        one_block, (zero_rows, zero_rows), jnp.arange(length // block_rows, dtype=jnp.int32)
    )
    return (query_grad.reshape(queries.shape), key_grad, value_grad)


def body(
    hidden_in,
    norm_gain,
    norm_shift,
    qkv_weight,
    qv_bias,
    out_weight,
    out_bias,
    up_weight,
    up_bias,
    down_weight,
    cotangent,
):
    local_rows = hidden_in.shape[0]
    tensor_size = lax.axis_size("tensor")
    length = local_rows * tensor_size
    local_width = qkv_weight.shape[2]
    local_heads = HEADS // tensor_size
    head_dim = local_width // local_heads
    block_rows = min(512, length)
    head_ids = lax.axis_index("tensor") * local_heads + jnp.arange(local_heads, dtype=jnp.int32)
    slopes = jnp.exp2(-8.0 * (head_ids.astype(jnp.float32) + 1.0) / HEADS)
    qkv_full, out_full, up_full, down_full = (
        lax.all_gather(qkv_weight, "dp", axis=1, tiled=True),
        lax.all_gather(out_weight, "dp", axis=1, tiled=True),
        lax.all_gather(up_weight, "dp", axis=0, tiled=True),
        lax.all_gather(down_weight, "dp", axis=1, tiled=True),
    )
    hidden = hidden_in.astype(jnp.float32)
    normed, scaled_one, inverse_one = layer_norm(hidden, norm_gain[0], norm_shift[0])
    normed_rows = lax.all_gather(normed.astype(jnp.bfloat16), "tensor", axis=0, tiled=True)
    projected = jnp.einsum("ld,cdw->clw", normed_rows, qkv_full, preferred_element_type=jnp.float32)
    queries = (
        (projected[0] + qv_bias[0]).astype(jnp.bfloat16).reshape(length, local_heads, head_dim)
    )
    key_rows = projected[1].astype(jnp.bfloat16).reshape(length, local_heads, head_dim)
    value_rows = (
        (projected[2] + qv_bias[1]).astype(jnp.bfloat16).reshape(length, local_heads, head_dim)
    )
    mixed_f32, logsums = attend_forward(queries, key_rows, value_rows, slopes, block_rows)
    mixed = mixed_f32.astype(jnp.bfloat16)
    piece = mixed
    attn_sum = lax.psum_scatter(
        jnp.dot(piece, out_full, preferred_element_type=jnp.float32),
        "tensor",
        scatter_dimension=0,
        tiled=True,
    )
    middle = hidden + attn_sum + out_bias[0]
    second, scaled_two, inverse_two = layer_norm(middle, norm_gain[1], norm_shift[1])
    second_rows = lax.all_gather(second.astype(jnp.bfloat16), "tensor", axis=0, tiled=True)
    upper = jnp.dot(second_rows, up_full, preferred_element_type=jnp.float32) + up_bias
    active = gelu_tanh(upper).astype(jnp.bfloat16)
    piece = active
    mlp_sum = lax.psum_scatter(
        jnp.dot(piece, down_full, preferred_element_type=jnp.float32).astype(jnp.bfloat16),
        "tensor",
        scatter_dimension=0,
        tiled=True,
    ).astype(jnp.float32)
    block_out = middle + mlp_sum + out_bias[1]
    qkv_back, out_back, up_back, down_back = (
        lax.all_gather(qkv_weight, "dp", axis=1, tiled=True),
        lax.all_gather(out_weight, "dp", axis=1, tiled=True),
        lax.all_gather(up_weight, "dp", axis=0, tiled=True),
        lax.all_gather(down_weight, "dp", axis=1, tiled=True),
    )
    grad_out = cotangent.astype(jnp.float32)
    grad_rows = lax.all_gather(cotangent, "tensor", axis=0, tiled=True)
    grad_down = lax.dot_general(
        active, grad_rows, (((0,), (0,)), ((), ())), preferred_element_type=jnp.float32
    )
    grad_active = lax.dot_general(
        grad_rows, down_back, (((1,), (1,)), ((), ())), preferred_element_type=jnp.float32
    )
    grad_upper = (grad_active * gelu_slope(upper)).astype(jnp.bfloat16)
    grad_up_bias = jnp.sum(grad_upper.astype(jnp.float32), axis=0)
    grad_up = lax.dot_general(
        second_rows, grad_upper, (((0,), (0,)), ((), ())), preferred_element_type=jnp.float32
    )
    piece = grad_upper
    grad_second = lax.psum_scatter(
        lax.dot_general(
            piece, up_back, (((1,), (1,)), ((), ())), preferred_element_type=jnp.float32
        ),
        "tensor",
        scatter_dimension=0,
        tiled=True,
    )
    grad_from_norm, gain_two, shift_two = norm_backward(
        grad_second, scaled_two, inverse_two, norm_gain[1]
    )
    grad_middle = grad_out + grad_from_norm
    attn_rows = lax.all_gather(grad_middle.astype(jnp.bfloat16), "tensor", axis=0, tiled=True)
    grad_out_w = lax.dot_general(
        mixed, attn_rows, (((0,), (0,)), ((), ())), preferred_element_type=jnp.float32
    )
    grad_mixed = lax.dot_general(
        attn_rows, out_back, (((1,), (1,)), ((), ())), preferred_element_type=jnp.float32
    )
    grad_mixed = grad_mixed.astype(jnp.bfloat16).reshape(length, local_heads, head_dim)
    query_grad, key_grad, value_grad = attend_backward(
        queries, key_rows, value_rows, grad_mixed, logsums, slopes, block_rows
    )
    query_low = query_grad.reshape(length, local_width).astype(jnp.bfloat16)
    key_low = key_grad.reshape(length, local_width).astype(jnp.bfloat16)
    value_low = value_grad.reshape(length, local_width).astype(jnp.bfloat16)
    stacked = jnp.stack([query_low, key_low, value_low])
    grad_qv = jnp.stack(
        [
            jnp.sum(query_low.astype(jnp.float32), axis=0),
            jnp.sum(value_low.astype(jnp.float32), axis=0),
        ]
    )
    grad_qkv_local = jnp.einsum(
        "ld,clw->cdw", normed_rows, stacked, preferred_element_type=jnp.float32
    )
    piece = stacked
    grad_normed = lax.psum_scatter(
        jnp.einsum("clw,cdw->ld", piece, qkv_back, preferred_element_type=jnp.float32).astype(
            jnp.bfloat16
        ),
        "tensor",
        scatter_dimension=0,
        tiled=True,
    ).astype(jnp.float32)
    grad_from_first, gain_one, shift_one = norm_backward(
        grad_normed, scaled_one, inverse_one, norm_gain[0]
    )
    grad_in = grad_middle + grad_from_first
    grad_qkv, grad_out_weight, grad_up_weight, grad_down_weight = (
        lax.psum_scatter(grad_qkv_local, "dp", scatter_dimension=1, tiled=True),
        lax.psum_scatter(grad_out_w, "dp", scatter_dimension=1, tiled=True),
        lax.psum_scatter(grad_up, "dp", scatter_dimension=0, tiled=True),
        lax.psum_scatter(grad_down, "dp", scatter_dimension=1, tiled=True),
    )
    grad_qv_bias, grad_up_bias_all = lax.psum((grad_qv, grad_up_bias), "dp")
    gain_local = jnp.stack([gain_one, gain_two])
    shift_local = jnp.stack([shift_one, shift_two])
    bias_local = jnp.stack([jnp.sum(grad_middle, axis=0), jnp.sum(grad_out, axis=0)])
    grad_norm_gain, grad_norm_shift, grad_out_bias = lax.psum(
        (gain_local, shift_local, bias_local), ("dp", "tensor")
    )
    return (
        block_out,
        grad_in,
        grad_norm_gain,
        grad_norm_shift,
        grad_qkv,
        grad_qv_bias,
        grad_out_weight,
        grad_out_bias,
        grad_up_weight,
        grad_up_bias_all,
        grad_down_weight,
    )


def solution(mesh):
    return jax.shard_map(
        body,
        mesh=mesh,
        in_specs=(
            P(("dp", "tensor"), None),
            P(),
            P(),
            P(None, "dp", "tensor"),
            P(None, "tensor"),
            P("tensor", "dp"),
            P(),
            P("dp", "tensor"),
            P("tensor"),
            P("tensor", "dp"),
            P(("dp", "tensor"), None),
        ),
        out_specs=(
            P(("dp", "tensor"), None),
            P(("dp", "tensor"), None),
            P(),
            P(),
            P(None, "dp", "tensor"),
            P(None, "tensor"),
            P("tensor", "dp"),
            P(),
            P("dp", "tensor"),
            P("tensor"),
            P("tensor", "dp"),
        ),
        check_vma=False,
    )
```

profile of v0, /device:TPU:0, one launch (start us, length us, event | category | flops | bytes accessed | tf_op | source)
XLA Modules:
  0.0 1269.2 jit_solution(10442887162435122413)
XLA Ops:
  17.9 33.2 %all_gather.30 = bf16[256,1024]{1,0:T(8,128)(2,1)} all-gather(bf16[256,128]{1,0:T(8,128)(2,1)S(1)} %copy-done.17), channel_id=1, replica_groups=mesh['dp'=8,'tensor'=4] {'dp'}, dimensions={1}, use_global_device_ids=true | all-gather | bytes 589824 | tf_op jit(solution)/shard_map/all_gather | solution.py:142
  51.1 11.6 all-gather.10.cloned.1.call-done
  62.6 35.7 %all-gather.8.cloned.1.call-done = bf16[2048,1024]{1,0:T(8,128)(2,1)} async-done(((bf16[512,1024]{1,0:T(8,128)(2,1)}), bf16[2048,1024]{1,0:T(8,128)(2,1)}) %all-gather.8.cloned.1.call-update) | async-done | bytes 4194320 | tf_op jit(solution)/shard_map/all_gather | solution.py:148
  98.3 5.7 fusion.48
  106.4 97.3 %while.28 = (s32[]{:T(128)}, bf16[4,512,256]{2,1,0:T(8,128)(2,1)}, f32[4,4,512]{2,1,0:T(4,128)S(1)}, s32[4]{0:T(128)S(1)}, bf16[2048,4,64]{0,2,1:T(8,128)(2,1)},...) while((s32[]{:T(128)}, bf16[4,512,256]{2,1,0:T(8,128)(2,1)}, ...), condition=%wide.region_5.6_spmd.clone, body=%wide.region_2.5_spmd.clone.sunk | while | flops 1153432064 | bytes 91822360 | solution.py:72
  108.9 6.4 fusion.136
  115.3 5.8 fusion.137
  121.1 8.8 fusion.138
  133.1 6.3 fusion.136
  139.5 5.8 fusion.137
  145.3 8.8 fusion.138
  157.3 6.4 fusion.136
  163.7 5.8 fusion.137
  169.5 8.8 fusion.138
  181.5 6.4 fusion.136
  187.9 5.8 fusion.137
  193.7 8.8 fusion.138
  203.7 5.8 fusion.80
  210.3 71.2 %reduce-scatter.9.cloned.1.call-done = f32[512,1024]{1,0:T(8,128)} async-done(((f32[2048,1024]{1,0:T(8,128)}), f32[512,1024]{1,0:T(8,128)}) %reduce-scatter.9.cloned.1.call-update) | async-done | bytes 2097168 | tf_op jit(solution)/shard_map/reduce_scatter | solution.py:160
  287.6 45.4 %all-gather.14.cloned.1.call-done = bf16[1024,1024]{1,0:T(8,128)(2,1)} async-done(((bf16[128,1024]{1,0:T(8,128)(2,1)}), bf16[1024,1024]{1,0:T(8,128)(2,1)}) %all-gather.14.cloned.1.call-update) | async-done | bytes 2097168 | tf_op jit(solution)/shard_map/all_gather | solution.py:143
  333.0 35.1 %all-gather.12.cloned.1.call-done = bf16[2048,1024]{1,0:T(8,128)(2,1)} async-done(((bf16[512,1024]{1,0:T(8,128)(2,1)}), bf16[2048,1024]{1,0:T(8,128)(2,1)}) %all-gather.12.cloned.1.call-update) | async-done | bytes 4194320 | tf_op jit(solution)/shard_map/all_gather | solution.py:168
  368.1 10.6 fusion.81
  378.7 42.6 %all-gather.16.cloned.1.call-done = bf16[1024,1024]{1,0:T(8,128)(2,1)} async-done(((bf16[1024,128]{1,0:T(8,128)(2,1)}), bf16[1024,1024]{1,0:T(8,128)(2,1)}) %all-gather.16.cloned.1.call-update) | async-done | bytes 2097168 | tf_op jit(solution)/shard_map/all_gather | solution.py:144
  421.3 34.3 %all-gather.18.cloned.1.call-done = bf16[2048,1024]{1,0:T(8,128)(2,1)} async-done(((bf16[512,1024]{1,0:T(8,128)(2,1)}), bf16[2048,1024]{1,0:T(8,128)(2,1)}) %all-gather.18.cloned.1.call-update) | async-done | bytes 4194320 | tf_op jit(solution)/shard_map/all_gather | solution.py:186
  455.6 13.8 %convert_reduce_fusion = (f32[1024]{0:T(1024)}, bf16[2048,1024]{1,0:T(8,128)(2,1)S(1)}) fusion(f32[2048,1024]{1,0:T(8,128)} %fusion.81, f32[1024]{0:T(1024)S(1)} %copy-done.32, bf16[2048,1024]{1,0:T(8,128)(2,1)} %all-gather.18.cloned.1.call-done, bf16[1024,1024]{1,0:T(8,128)(2,1)} %all-gather.16.cloned.1.call-done), kind=kOutput, calls=%fused_computation.58 | convolution fusion | flops 4341103616 | bytes 18882560 | tf_op jit(solution)/shard_map/dot_general | solution.py:190
  471.4 8.4 fusion.82
  479.9 12.2 convolution_convert_fusion
  492.2 59.6 %reduce-scatter.13.cloned.1.call-done = f32[512,1024]{1,0:T(8,128)} async-done(((f32[2048,1024]{1,0:T(8,128)}), f32[512,1024]{1,0:T(8,128)}) %reduce-scatter.13.cloned.1.call-update) | async-done | bytes 2097168 | tf_op jit(solution)/shard_map/reduce_scatter | solution.py:199
  555.4 43.4 %reduce-scatter.11.cloned.1.call-done = bf16[512,1024]{1,0:T(8,128)(2,1)} async-done(((bf16[2048,1024]{1,0:T(8,128)(2,1)}), bf16[512,1024]{1,0:T(8,128)(2,1)}) %reduce-scatter.11.cloned.1.call-update) | async-done | bytes 1048592 | tf_op jit(solution)/shard_map/reduce_scatter | solution.py:172
  598.8 4.6 fusion.73
  606.0 34.6 %all-gather.20.cloned.1.call-done = bf16[2048,1024]{1,0:T(8,128)(2,1)} async-done(((bf16[512,1024]{1,0:T(8,128)(2,1)}), bf16[2048,1024]{1,0:T(8,128)(2,1)}) %all-gather.20.cloned.1.call-update) | async-done | bytes 4194320 | tf_op jit(solution)/shard_map/all_gather | solution.py:211
  640.5 4.4 convolution_convert_fusion.1
  645.0 220.1 %while.29 = (s32[]{:T(128)}, f32[2048,4,64]{0,2,1:T(8,128)}, f32[2048,4,64]{0,2,1:T(8,128)}, bf16[4,512,4,64]{1,3,2,0:T(8,128)(2,1)}, s32[4]{0:T(128)S(1)}, /*in...) while((s32[]{:T(128)}, f32[2048,4,64]{0,2,1:T(8,128)}, ...), condition=%wide.region_15.16_spmd.clone, body=%wide.region_13.15_spmd.clone.sunk | while | flops 2737437184 | bytes 216578384 | solution.py:112
  649.4 9.1 fusion.148
  658.5 14.1 %multiply_reduce_fusion.6 = (f32[4,512]{1,0:T(4,128)S(1)}, f32[4,512,2048]{2,1,0:T(8,128)}) fusion(f32[4,512,2048]{2,1,0:T(8,128)} %fusion.148, f32[4,512]{1,0:T(4,128)S(1)} %dynamic-slice_bitcast_fusion.2, f32[512,2048]{1,0:T(8,128)S(1)} %fusion.149, f32[4]{0:T(128)S(1)} %multiply_exponential_fusion.5, ...), kind=kOutput, calls=%fused_computation.21.clone.1 | convolution fusion | flops 566228992 | bytes 40124436 | tf_op jit(solution)/shard_map/while/body/eval_jaxpr/qhd,khd->hqk/dot_general | solution.py:43
  672.6 11.5 multiply_convert_fusion.5
  703.3 9.1 fusion.148
  712.4 14.1 %multiply_reduce_fusion.6 = (f32[4,512]{1,0:T(4,128)S(1)}, f32[4,512,2048]{2,1,0:T(8,128)}) fusion(f32[4,512,2048]{2,1,0:T(8,128)} %fusion.148, f32[4,512]{1,0:T(4,128)S(1)} %dynamic-slice_bitcast_fusion.2, f32[512,2048]{1,0:T(8,128)S(1)} %fusion.149, f32[4]{0:T(128)S(1)} %multiply_exponential_fusion.5, ...), kind=kOutput, calls=%fused_computation.21.clone.1 | convolution fusion | flops 566228992 | bytes 40124436 | tf_op jit(solution)/shard_map/while/body/eval_jaxpr/qhd,khd->hqk/dot_general | solution.py:43
  726.4 11.5 multiply_convert_fusion.5
  741.8 4.6 fusion.152
  749.8 4.6 fusion.151
  758.7 9.1 fusion.148
  767.8 14.1 %multiply_reduce_fusion.6 = (f32[4,512]{1,0:T(4,128)S(1)}, f32[4,512,2048]{2,1,0:T(8,128)}) fusion(f32[4,512,2048]{2,1,0:T(8,128)} %fusion.148, f32[4,512]{1,0:T(4,128)S(1)} %dynamic-slice_bitcast_fusion.2, f32[512,2048]{1,0:T(8,128)S(1)} %fusion.149, f32[4]{0:T(128)S(1)} %multiply_exponential_fusion.5, ...), kind=kOutput, calls=%fused_computation.21.clone.1 | convolution fusion | flops 566228992 | bytes 40124436 | tf_op jit(solution)/shard_map/while/body/eval_jaxpr/qhd,khd->hqk/dot_general | solution.py:43
  781.8 11.5 multiply_convert_fusion.5
  797.2 4.6 fusion.152
  805.1 4.6 fusion.151
  814.0 9.1 fusion.148
  823.1 14.1 %multiply_reduce_fusion.6 = (f32[4,512]{1,0:T(4,128)S(1)}, f32[4,512,2048]{2,1,0:T(8,128)}) fusion(f32[4,512,2048]{2,1,0:T(8,128)} %fusion.148, f32[4,512]{1,0:T(4,128)S(1)} %dynamic-slice_bitcast_fusion.2, f32[512,2048]{1,0:T(8,128)S(1)} %fusion.149, f32[4]{0:T(128)S(1)} %multiply_exponential_fusion.5, ...), kind=kOutput, calls=%fused_computation.21.clone.1 | convolution fusion | flops 566228992 | bytes 40124436 | tf_op jit(solution)/shard_map/while/body/eval_jaxpr/qhd,khd->hqk/dot_general | solution.py:43
  837.2 11.5 multiply_convert_fusion.5
  852.5 4.6 fusion.152
  860.5 4.6 fusion.151
  872.8 4.5 reshape.210
  878.9 8.5 fusion.67
  887.4 6.3 bitcast_convert_fusion
  894.5 12.5 fusion.72
  907.3 10.1 fusion.84
  918.7 4.5 fusion.83
  925.0 22.5 %all-reduce.1 = (f32[2,256]{1,0:T(2,128)}, f32[1024]{0:T(1024)}) all-reduce(f32[2,256]{1,0:T(2,128)S(1)} %pad_maximum_fusion.6, f32[1024]{0:T(1024)S(1)} %copy-done.30), channel_id=1, replica_groups=mesh['dp'=8,'tensor'=4] {'dp'}, use_global_device_ids=true, to_apply=%region_28.29 | all-reduce | flops 1536 | bytes 12288 | tf_op jit(solution)/shard_map/psum | solution.py:254
  947.5 15.4 %reduce-scatter.17.cloned.1.call-done = f32[3,128,256]{1,2,0:T(8,128)} async-done(((f32[3,1024,256]{1,2,0:T(8,128)}), f32[3,128,256]{1,2,0:T(8,128)}) %reduce-scatter.17.cloned.1.call-update) | async-done | bytes 393232 | tf_op jit(solution)/shard_map/reduce_scatter | solution.py:249
  964.8 44.3 %reduce-scatter.15.cloned.1.call-done = bf16[512,1024]{1,0:T(8,128)(2,1)} async-done(((bf16[2048,1024]{1,0:T(8,128)(2,1)}), bf16[512,1024]{1,0:T(8,128)(2,1)}) %reduce-scatter.15.cloned.1.call-update) | async-done | bytes 1048592 | tf_op jit(solution)/shard_map/reduce_scatter | solution.py:236
  1011.4 42.4 %all-reduce = (f32[2,1024]{1,0:T(2,128)}, f32[2,1024]{1,0:T(2,128)}, f32[2,1024]{1,0:T(2,128)}) all-reduce(f32[2,1024]{1,0:T(2,128)S(1)} %pad_maximum_fusion.3, f32[2,1024]{1,0:T(2,128)S(1)} %pad_maximum_fusion.4, f32[2,1024]{1,0:T(2,128)S(1)} %pad_maximum_fusion.5), channel_id=1, replica_groups=mesh['dp'=8,'tensor'=4] {'dp','tensor'}, use_global_device_ids=true, to_apply=%region_21.22 | all-reduce | flops 6144 | bytes 49152 | tf_op jit(solution)/shard_map/psum | solution.py:258
  1057.1 45.7 %reduce-scatter.23.cloned.1.call-done = f32[1024,128]{1,0:T(8,128)} async-done(((f32[1024,1024]{1,0:T(8,128)}), f32[1024,128]{1,0:T(8,128)}) %reduce-scatter.23.cloned.1.call-update) | async-done | bytes 524304 | tf_op jit(solution)/shard_map/reduce_scatter | solution.py:252
  1102.8 92.2 %reduce-scatter.21.cloned.1.call-done = f32[128,1024]{1,0:T(8,128)} async-done(((f32[1024,1024]{1,0:T(8,128)}), f32[128,1024]{1,0:T(8,128)}) %reduce-scatter.21.cloned.1.call-update) | async-done | bytes 524304 | tf_op jit(solution)/shard_map/reduce_scatter | solution.py:251
  1195.0 67.4 %reduce-scatter.19.cloned.1.call-done = f32[256,128]{1,0:T(8,128)} async-done(((f32[256,1024]{1,0:T(8,128)}), f32[256,128]{1,0:T(8,128)}) %reduce-scatter.19.cloned.1.call-update) | async-done | bytes 131088 | tf_op jit(solution)/shard_map/reduce_scatter | solution.py:250
  (222 shorter events, 102.4 us)
Async XLA Ops:
  7.2 10.5 copy-start.31
  7.2 10.7 copy-start.17
  7.2 55.4 %all-gather.10.cloned.1.call-start = ((), (), s32[]{:S(2)}) async-start(), calls=%async_computation.9 | async-start | bytes 1769472 | tf_op jit(solution)/shard_map/all_gather | solution.py:141
  9.0 89.3 %all-gather.8.cloned.1.call-start = ((), (), s32[]{:S(2)}) async-start(), calls=%async_computation.8 | async-start | bytes 5242880 | tf_op jit(solution)/shard_map/all_gather | solution.py:148
  10.5 4.4 copy-start.20
  12.2 2.8 copy-start.22
  13.5 1.4 copy-start.18
  17.6 263.9 %reduce-scatter.9.cloned.1.call-start = ((), (), s32[]{:S(2)}) async-start(), calls=%async_computation.10 | async-start | bytes 10485760 | tf_op jit(solution)/shard_map/reduce_scatter | solution.py:160
  108.9 6.4 copy-start.1
  133.1 6.4 copy-start.1
  157.3 6.4 copy-start.1
  181.5 6.4 copy-start.1
  209.6 0.7 copy-start.29
  209.6 71.9 %copy-start.4 = (bf16[512,1024]{1,0:T(8,128)(2,1)S(1)}, bf16[512,1024]{1,0:T(8,128)(2,1)}, u32[]{:S(2)}) copy-start(bf16[512,1024]{1,0:T(8,128)(2,1)} %param.15) | copy-start | bytes 3145732
  209.6 75.2 %copy-start.16 = (f32[1,1024]{1,0:T(1,128)S(1)}, f32[1,1024]{1,0:T(1,128)}, u32[]{:S(2)}) copy-start(f32[1,1024]{1,0:T(1,128)} %get-tuple-element.267) | copy-start | bytes 12292
  209.6 75.2 %copy-start.28 = (f32[1,1024]{1,0:T(1,128)S(1)}, f32[1,1024]{1,0:T(1,128)}, u32[]{:S(2)}) copy-start(f32[1,1024]{1,0:T(1,128)} %get-tuple-element.269) | copy-start | bytes 12292
  209.6 123.4 %all-gather.14.cloned.1.call-start = ((), (), s32[]{:S(2)}) async-start(), calls=%async_computation.12 | async-start | bytes 2359296 | tf_op jit(solution)/shard_map/all_gather | solution.py:143
  210.2 157.9 %all-gather.12.cloned.1.call-start = ((), (), s32[]{:S(2)}) async-start(), calls=%async_computation.11 | async-start | bytes 5242880 | tf_op jit(solution)/shard_map/all_gather | solution.py:168
  283.5 1.3 copy-start.3
  286.2 135.1 %all-gather.16.cloned.1.call-start = ((), (), s32[]{:S(2)}) async-start(), calls=%async_computation.13 | async-start | bytes 2359296 | tf_op jit(solution)/shard_map/all_gather | solution.py:144
  286.8 168.9 %all-gather.18.cloned.1.call-start = ((), (), s32[]{:S(2)}) async-start(), calls=%async_computation.15 | async-start | bytes 5242880 | tf_op jit(solution)/shard_map/all_gather | solution.py:186
  287.5 168.1 %copy-start.32 = (f32[1024]{0:T(1024)S(1)}, f32[1024]{0:T(1024)}, u32[]{:S(2)}) copy-start(f32[1024]{0:T(1024)} %param.23) | copy-start | bytes 12292
  287.5 264.2 %reduce-scatter.13.cloned.1.call-start = ((), (), s32[]{:S(2)}) async-start(), calls=%async_computation.16 | async-start | bytes 10485760 | tf_op jit(solution)/shard_map/reduce_scatter | solution.py:199
  469.4 2.0 copy-start.34
  479.9 118.9 %reduce-scatter.11.cloned.1.call-start = ((), (), s32[]{:S(2)}) async-start(), calls=%async_computation.14 | async-start | bytes 5242880 | tf_op jit(solution)/shard_map/reduce_scatter | solution.py:172
  492.1 106.7 %copy-start.9 = (bf16[512,1024]{1,0:T(8,128)(2,1)S(1)}, bf16[512,1024]{1,0:T(8,128)(2,1)}, u32[]{:S(2)}) copy-start(bf16[512,1024]{1,0:T(8,128)(2,1)} %param.25) | copy-start | bytes 3145732
  492.2 148.4 %all-gather.20.cloned.1.call-start = ((), (), s32[]{:S(2)}) async-start(), calls=%async_computation.17 | async-start | bytes 5242880 | tf_op jit(solution)/shard_map/all_gather | solution.py:211
  603.4 1.3 copy-start.7
  603.4 37.1 %copy-start.11 = (bf16[256,1024]{1,0:T(8,128)(2,1)S(1)}, bf16[256,1024]{1,0:T(8,128)(2,1)}, u32[]{:S(2)}) copy-start(bf16[256,1024]{1,0:T(8,128)(2,1)} %all_gather.30) | copy-start | bytes 1572868
  605.9 39.1 %copy-start.6 = (bf16[2048,4,64]{0,2,1:T(8,128)(2,1)S(1)}, bf16[2048,4,64]{0,2,1:T(8,128)(2,1)}, u32[]{:S(2)}) copy-start(bf16[2048,4,64]{0,2,1:T(8,128)(2,1)} %get-tuple-element.501) | copy-start | bytes 3145732
  605.9 357.0 %reduce-scatter.17.cloned.1.call-start = ((), (), s32[]{:S(2)}) async-start(), calls=%async_computation.19 | async-start | bytes 3538944 | tf_op jit(solution)/shard_map/reduce_scatter | solution.py:249
  672.6 15.4 %copy-start = (f32[4,512,2048]{2,1,0:T(8,128)S(1)}, f32[4,512,2048]{2,1,0:T(8,128)}, u32[]{:S(2)}) copy-start(f32[4,512,2048]{2,1,0:T(8,128)} %get-tuple-element.397) | copy-start | bytes 50331652 | tf_op jit(solution)/shard_map/while
  726.4 15.4 %copy-start = (f32[4,512,2048]{2,1,0:T(8,128)S(1)}, f32[4,512,2048]{2,1,0:T(8,128)}, u32[]{:S(2)}) copy-start(f32[4,512,2048]{2,1,0:T(8,128)} %get-tuple-element.397) | copy-start | bytes 50331652 | tf_op jit(solution)/shard_map/while
  781.8 15.4 %copy-start = (f32[4,512,2048]{2,1,0:T(8,128)S(1)}, f32[4,512,2048]{2,1,0:T(8,128)}, u32[]{:S(2)}) copy-start(f32[4,512,2048]{2,1,0:T(8,128)} %get-tuple-element.397) | copy-start | bytes 50331652 | tf_op jit(solution)/shard_map/while
  837.1 15.4 %copy-start = (f32[4,512,2048]{2,1,0:T(8,128)S(1)}, f32[4,512,2048]{2,1,0:T(8,128)}, u32[]{:S(2)}) copy-start(f32[4,512,2048]{2,1,0:T(8,128)} %get-tuple-element.397) | copy-start | bytes 50331652 | tf_op jit(solution)/shard_map/while
  865.1 5.2 copy-start.10
  867.9 9.5 copy-start.2
  878.9 8.5 copy-start.13
  878.9 8.5 copy-start.14
  878.9 8.6 copy-start.15
  887.4 121.7 %reduce-scatter.15.cloned.1.call-start = ((), (), s32[]{:S(2)}) async-start(), calls=%async_computation.18 | async-start | bytes 5242880 | tf_op jit(solution)/shard_map/reduce_scatter | solution.py:236
  893.8 0.7 copy-start.33
  893.8 209.0 %reduce-scatter.23.cloned.1.call-start = ((), (), s32[]{:S(2)}) async-start(), calls=%async_computation.22 | async-start | bytes 4718592 | tf_op jit(solution)/shard_map/reduce_scatter | solution.py:252
  907.0 288.0 %reduce-scatter.21.cloned.1.call-start = ((), (), s32[]{:S(2)}) async-start(), calls=%async_computation.21 | async-start | bytes 4718592 | tf_op jit(solution)/shard_map/reduce_scatter | solution.py:251
  917.4 1.2 copy-start.12
  917.5 5.7 copy-start.26
  917.5 5.7 copy-start.27
  917.5 7.6 copy-start.30
  917.5 91.6 %copy-start.5 = (bf16[512,1024]{1,0:T(8,128)(2,1)S(1)}, bf16[512,1024]{1,0:T(8,128)(2,1)}, u32[]{:S(2)}) copy-start(bf16[512,1024]{1,0:T(8,128)(2,1)} %param.15) | copy-start | bytes 3145732
  917.5 91.6 %copy-start.19 = (f32[1,1024]{1,0:T(1,128)S(1)}, f32[1,1024]{1,0:T(1,128)}, u32[]{:S(2)}) copy-start(f32[1,1024]{1,0:T(1,128)} %copy-done.18) | copy-start | bytes 12292
  917.5 91.6 %copy-start.21 = (f32[512]{0:T(512)S(1)}, f32[512]{0:T(512)}, u32[]{:S(2)}) copy-start(f32[512]{0:T(512)} %copy-done.20) | copy-start | bytes 6148
  917.5 91.6 %copy-start.23 = (f32[512]{0:T(512)S(1)}, f32[512]{0:T(512)}, u32[]{:S(2)}) copy-start(f32[512]{0:T(512)} %copy-done.22) | copy-start | bytes 6148
  917.5 344.9 %reduce-scatter.19.cloned.1.call-start = ((), (), s32[]{:S(2)}) async-start(), calls=%async_computation.20 | async-start | bytes 1179648 | tf_op jit(solution)/shard_map/reduce_scatter | solution.py:250
  923.1 88.2 %copy-start.25 = (f32[1024]{0:T(1024)S(1)}, f32[1024]{0:T(1024)}, u32[]{:S(2)}) copy-start(f32[1024]{0:T(1024)} %get-tuple-element.198) | copy-start | bytes 12292
  923.1 88.2 %copy-start.24 = (f32[1024]{0:T(1024)S(1)}, f32[1024]{0:T(1024)}, u32[]{:S(2)}) copy-start(f32[1024]{0:T(1024)} %get-tuple-element.203) | copy-start | bytes 12292
  923.2 130.7 %copy-start.8 = (f32[512,1024]{1,0:T(8,128)S(1)}, f32[512,1024]{1,0:T(8,128)}, u32[]{:S(2)}) copy-start(f32[512,1024]{1,0:T(8,128)} %copy-done.7) | copy-start | bytes 6291460
Sparse Core Ops, SparseCore 0:
  10.6 51.9 all-gather.9
  64.8 33.5 all-gather.7
  209.7 71.7 reduce-scatter.8
  283.7 49.2 all-gather.13
  335.1 32.9 all-gather.11
  370.2 51.0 all-gather.15
  422.9 32.6 all-gather.17
  480.0 71.6 reduce-scatter.12
  554.3 44.4 reduce-scatter.10
  606.0 34.4 all-gather.19
  887.5 75.3 reduce-scatter.16
  965.4 43.6 reduce-scatter.14
  1013.3 89.5 reduce-scatter.22
  1107.3 87.6 reduce-scatter.20
  1198.9 63.5 reduce-scatter.18
where the time goes:
time: 1270 us
  waiting for transfers between devices  680 us (54%)
  matrix products  305 us (24%)
  other arithmetic  109 us (9%)
  blocking collectives  98.1 us (8%)
  local copies, waits for them, and re-layouts  48.1 us (4%)
  between operations  14.6 us (1%)
  loops' own time  14.2 us (1%)
    reduce_scatter x1, waiting for transfers between devices, body(): lax.psum_scatter(grad_up, 'dp', scatter_dimension=0, tiled=True)  92.2 us
    dot_general x8, matrix products, block_scores(): jnp.einsum('qhd,khd->hqk', query_block, key_rows, preferred_element_type=...  81.6 us
    reduce_scatter x1, waiting for transfers between devices, body(): lax.psum_scatter(jnp.dot(piece, out_full, preferred_element_type=jnp.floa...  71.2 us
    reduce_scatter x1, waiting for transfers between devices, body(): lax.psum_scatter(grad_out_w, 'dp', scatter_dimension=1, tiled=True)  67.4 us
    reduce_scatter x1, waiting for transfers between devices, body(): lax.psum_scatter(lax.dot_general(piece, up_back, (((1,), (1,)), ((), ()))...  59.6 us
    convert_element_type x4, other arithmetic, one_block(): (attention * (grad_attention - centering)).astype(jnp.bfloat16)  45.9 us
    reduce_scatter x1, waiting for transfers between devices, body(): lax.psum_scatter(grad_down, 'dp', scatter_dimension=1, tiled=True)  45.7 us
    all_gather x1, waiting for transfers between devices, body(): lax.all_gather(up_weight, 'dp', axis=0, tiled=True)  45.4 us
  transfers between devices with their start and end apart: 15, of which 15 were waited for; matrix products, arithmetic and copies ran while one was open for 6% of the time, Pallas kernels for 0%

commit v1 on v0

v1 whole, which is shorter than its diff:
```python
import functools
import math

import jax
import jax.numpy as jnp
from jax import lax
from jax.experimental import pallas as pl
from jax.experimental.pallas import tpu as pltpu
from jax.sharding import PartitionSpec as P

HEADS = 16
LOG2E = 1.4426950408889634
NEG = -1e30
BF16 = jnp.bfloat16
F32 = jnp.float32


def layer_norm(values, norm_gain, norm_shift):
    average = jnp.mean(values, axis=-1, keepdims=True)
    centered = values - average
    inverse = lax.rsqrt(jnp.mean(centered * centered, axis=-1, keepdims=True) + 1e-05)
    scaled = centered * inverse
    return (scaled * norm_gain + norm_shift, scaled, inverse)


def norm_backward(gradient, scaled, inverse, norm_gain):
    grad_scaled = gradient * norm_gain
    grad_mean = jnp.mean(grad_scaled, axis=-1, keepdims=True)
    grad_proj = jnp.mean(grad_scaled * scaled, axis=-1, keepdims=True)
    grad_input = inverse * (grad_scaled - grad_mean - scaled * grad_proj)
    return (grad_input, jnp.sum(gradient * scaled, axis=0), jnp.sum(gradient, axis=0))


def gelu_both(values):
    square = values * values
    tangent = jnp.tanh(0.7978845608 * values * (1.0 + 0.044715 * square))
    half = 0.5 * (1.0 + tangent)
    slope = half + 0.5 * values * (1.0 - tangent * tangent) * 0.7978845608 * (
        1.0 + 3.0 * 0.044715 * square
    )
    return values * half, slope


def fill_bias(bias, masked, slope):
    size = bias.shape[0]
    key = lax.broadcasted_iota(jnp.int32, (size, size), 0)
    query = lax.broadcasted_iota(jnp.int32, (size, size), 1)
    value = key.astype(F32) * slope
    bias[...] = value
    masked[...] = jnp.where(key <= query, value, NEG)


def head_rows(block, head):
    half = block.shape[0] // 2
    rows = lax.broadcasted_iota(jnp.int32, block.shape, 0)
    keep = (rows < half) if head == 0 else (rows >= half)
    return jnp.where(keep, block, jnp.zeros_like(block))


def forward_kernel(
    place, slope_ref, q_ref, k_ref, v_ref, mixed_ref, full_ref, log_ref, bias, masked, values_t, *, scale
):
    pair = pl.program_id(0)
    query_block = pl.program_id(1)
    me = place[0]
    size = bias.shape[1]
    half = q_ref.shape[0] // 2

    @pl.when(query_block == 0)
    def _():
        values_t[...] = v_ref[...].T
        for head in range(2):
            fill_bias(bias.at[head], masked.at[head], slope_ref[2 * pair + head])

    outputs = []
    logs = []
    for head in range(2):
        step = slope_ref[2 * pair + head] * size
        queries = head_rows(q_ref[...], head)

        def block(key_block, carry, bias_block, head=head, step=step, queries=queries):
            top, total, acc = carry
            at = pl.multiple_of((key_block ^ me) * size, size)
            raw = jnp.dot(k_ref[pl.ds(at, size), :], queries, preferred_element_type=F32)
            scores = raw * scale + bias_block
            base = key_block.astype(F32) * step
            new_top = jnp.maximum(top, jnp.max(scores, axis=0, keepdims=True) + base)
            weights = jnp.exp2(scores - (new_top - base))
            fade = jnp.exp2(top - new_top)
            total = total * fade + jnp.sum(weights, axis=0, keepdims=True)
            rows = values_t[head * half : (head + 1) * half, pl.ds(at, size)]
            acc = acc * fade + jnp.dot(rows, weights.astype(BF16), preferred_element_type=F32)
            return new_top, total, acc

        start = (
            jnp.full((1, size), NEG, F32),
            jnp.zeros((1, size), F32),
            jnp.zeros((half, size), F32),
        )
        carry = lax.fori_loop(
            0, query_block, lambda i, c, head=head, block=block: block(i, c, bias[head]), start
        )
        top, total, acc = block(query_block, carry, masked[head])
        outputs.append(acc / total)
        logs.append(top + jnp.log2(total))
    result = jnp.concatenate(outputs, axis=0)
    full_ref[...] = result
    mixed_ref[...] = result.astype(BF16)
    log_ref[0] = jnp.concatenate(logs, axis=0)


def backward_kernel(
    place,
    slope_ref,
    q_ref,
    k_ref,
    v_ref,
    g_ref,
    full_ref,
    log_ref,
    gq_ref,
    gk_ref,
    gv_ref,
    bias,
    masked,
    gq_acc,
    delta,
    *,
    scale,
    factor,
):
    pair = pl.program_id(0)
    key_block = pl.program_id(1)
    blocks = pl.num_programs(1)
    me = place[0]
    size = bias.shape[1]
    half = q_ref.shape[0] // 2

    @pl.when(key_block == 0)
    def _():
        gq_acc[...] = jnp.zeros_like(gq_acc)
        for head in range(2):
            fill_bias(bias.at[head], masked.at[head], slope_ref[2 * pair + head])
            rows = slice(head * half, (head + 1) * half)
            delta[head : head + 1, :] = jnp.sum(
                g_ref[rows, :].astype(F32) * full_ref[rows, :], axis=0, keepdims=True
            )

    keys = k_ref[...]
    keys_t = keys.T
    values = v_ref[...]
    grad_k = jnp.zeros(keys.shape, F32)
    grad_v = jnp.zeros(keys.shape, F32)
    for head in range(2):
        base = key_block.astype(F32) * (slope_ref[2 * pair + head] * size)
        rows = slice(head * half, (head + 1) * half)

        def block(query_block, carry, bias_block, head=head, base=base, rows=rows):
            grad_k, grad_v = carry
            at = pl.multiple_of((query_block ^ me) * size, size)
            queries = head_rows(q_ref[:, pl.ds(at, size)], head)
            grads = head_rows(g_ref[:, pl.ds(at, size)], head)
            raw = jnp.dot(keys, queries, preferred_element_type=F32)
            log = log_ref[0, head : head + 1, pl.ds(at, size)] - base
            weights = jnp.exp2(raw * scale + (bias_block - log))
            along = jnp.dot(values, grads, preferred_element_type=F32)
            change = (weights * (along - delta[head : head + 1, pl.ds(at, size)])).astype(BF16)
            contract = (((1,), (1,)), ((), ()))
            grad_v = grad_v + lax.dot_general(
                weights.astype(BF16), grads, contract, preferred_element_type=F32
            )
            grad_k = grad_k + lax.dot_general(change, queries, contract, preferred_element_type=F32)
            gq_acc[rows, pl.ds(at, size)] += jnp.dot(
                keys_t[rows, :], change, preferred_element_type=F32
            )
            return grad_k, grad_v

        carry = block(key_block, (grad_k, grad_v), masked[head])
        grad_k, grad_v = lax.fori_loop(
            key_block + 1, blocks, lambda i, c, head=head, block=block: block(i, c, bias[head]), carry
        )
    gk_ref[...] = (grad_k * factor).astype(BF16)
    gv_ref[...] = grad_v.astype(BF16)

    @pl.when(key_block == blocks - 1)
    def _():
        gq_ref[...] = (gq_acc[...] * factor).astype(BF16)


def attend_forward(place, slopes, queries_t, keys, values, size, head_dim):
    width, length = queries_t.shape
    wide = 2 * head_dim
    pairs, blocks = width // wide, length // size
    along_q = pl.BlockSpec((wide, size), lambda p, i, me, s: (p, i ^ me[0]))
    whole = pl.BlockSpec((length, wide), lambda p, i, me, s: (0, p))
    return pl.pallas_call(
        functools.partial(forward_kernel, scale=LOG2E / math.sqrt(head_dim)),
        grid_spec=pltpu.PrefetchScalarGridSpec(
            num_scalar_prefetch=2,
            grid=(pairs, blocks),
            in_specs=[along_q, whole, whole],
            out_specs=[
                along_q,
                along_q,
                pl.BlockSpec((1, 2, size), lambda p, i, me, s: (p, 0, i ^ me[0])),
            ],
            scratch_shapes=[
                pltpu.VMEM((2, size, size), F32),
                pltpu.VMEM((2, size, size), F32),
                pltpu.VMEM((wide, length), BF16),
            ],
        ),
        out_shape=[
            jax.ShapeDtypeStruct((width, length), BF16),
            jax.ShapeDtypeStruct((width, length), F32),
            jax.ShapeDtypeStruct((pairs, 2, length), F32),
        ],
        compiler_params=pltpu.CompilerParams(vmem_limit_bytes=48 * 2**20),
        cost_estimate=pl.CostEstimate(
            flops=20 * 10**9, bytes_accessed=8 * 2**20, transcendentals=10**7
        ),
        name="attend_forward",
    )(place, slopes, queries_t, keys, values)


def attend_backward(place, slopes, queries_t, keys, values, grads_t, full, logs, size, head_dim):
    width, length = queries_t.shape
    wide = 2 * head_dim
    pairs, blocks = width // wide, length // size
    along_k = pl.BlockSpec((size, wide), lambda p, i, me, s: (i ^ me[0], p))
    whole = pl.BlockSpec((wide, length), lambda p, i, me, s: (p, 0))
    return pl.pallas_call(
        functools.partial(
            backward_kernel, scale=LOG2E / math.sqrt(head_dim), factor=1.0 / math.sqrt(head_dim)
        ),
        grid_spec=pltpu.PrefetchScalarGridSpec(
            num_scalar_prefetch=2,
            grid=(pairs, blocks),
            in_specs=[
                whole,
                along_k,
                along_k,
                whole,
                whole,
                pl.BlockSpec((1, 2, length), lambda p, i, me, s: (p, 0, 0)),
            ],
            out_specs=[whole, along_k, along_k],
            scratch_shapes=[
                pltpu.VMEM((2, size, size), F32),
                pltpu.VMEM((2, size, size), F32),
                pltpu.VMEM((wide, length), F32),
                pltpu.VMEM((2, length), F32),
            ],
        ),
        out_shape=[
            jax.ShapeDtypeStruct((width, length), BF16),
            jax.ShapeDtypeStruct((length, width), BF16),
            jax.ShapeDtypeStruct((length, width), BF16),
        ],
        compiler_params=pltpu.CompilerParams(vmem_limit_bytes=48 * 2**20),
        cost_estimate=pl.CostEstimate(
            flops=40 * 10**9, bytes_accessed=12 * 2**20, transcendentals=10**7
        ),
        name="attend_backward",
    )(place, slopes, queries_t, keys, values, grads_t, full, logs)


def swap(value, axis, distance):
    size = lax.axis_size(axis)
    return lax.ppermute(value, axis, [(i, i ^ distance) for i in range(size)])


def gather_blocks(value):
    far = swap(value, "tensor", 2)
    near = swap(value, "tensor", 1)
    return [value, near, far, swap(far, "tensor", 1)]


def scatter_blocks(parts):
    far = parts[2].astype(F32) + swap(parts[3], "tensor", 1).astype(F32)
    near = parts[0].astype(F32) + swap(parts[1], "tensor", 1).astype(F32)
    return near + swap(far.astype(BF16), "tensor", 2).astype(F32)


def exchange_blocks(parts):
    return [parts[0]] + [swap(parts[j], "tensor", j) for j in range(1, 4)]


def sum_over(value, axes):
    for axis in axes:
        distance = 1
        while distance < lax.axis_size(axis):
            value = value + swap(value, axis, distance)
            distance *= 2
    return value


def rows_of(value, count):
    size = value.shape[0] // count
    return [value[i * size : (i + 1) * size] for i in range(count)]


def dot(a, b, ca, cb):
    return lax.dot_general(a, b, (((ca,), (cb,)), ((), ())), preferred_element_type=F32)


def body(
    hidden_in,
    norm_gain,
    norm_shift,
    qkv_weight,
    qv_bias,
    out_weight,
    out_bias,
    up_weight,
    up_bias,
    down_weight,
    cotangent,
):
    local_rows = hidden_in.shape[0]
    tensor_size = lax.axis_size("tensor")
    dp_size = lax.axis_size("dp")
    local_width = qkv_weight.shape[2]
    local_heads = HEADS // tensor_size
    head_dim = local_width // local_heads
    me = lax.axis_index("tensor").astype(jnp.int32)
    place = me.reshape(1)
    head_ids = me * local_heads + jnp.arange(local_heads, dtype=jnp.int32)
    slopes = jnp.exp2(-8.0 * (head_ids.astype(F32) + 1.0) / HEADS) * LOG2E

    qkv_full = lax.all_gather(qkv_weight, "dp", axis=1, tiled=True)
    out_mine = lax.all_gather(out_weight, "dp", axis=1, tiled=True)
    up_full = lax.all_gather(up_weight, "dp", axis=0, tiled=True)
    down_full = lax.all_gather(down_weight, "dp", axis=1, tiled=True)

    hidden = hidden_in.astype(F32)
    normed, scaled_one, inverse_one = layer_norm(hidden, norm_gain[0], norm_shift[0])
    normed_rows = jnp.concatenate(gather_blocks(normed.astype(BF16)), axis=0)
    grad_rows = jnp.concatenate(gather_blocks(cotangent), axis=0)
    out_full = jnp.concatenate(gather_blocks(out_mine), axis=0)

    queries_t = (dot(qkv_full[0], normed_rows, 0, 1) + qv_bias[0][:, None]).astype(BF16)
    keys = dot(normed_rows, qkv_full[1], 1, 0).astype(BF16)
    values = (dot(normed_rows, qkv_full[2], 1, 0) + qv_bias[1]).astype(BF16)
    mixed_t, mixed_full, logs = attend_forward(
        place, slopes, queries_t, keys, values, local_rows, head_dim
    )
    mixed_parts = [
        mixed_t[:, j * local_rows : (j + 1) * local_rows] for j in range(tensor_size)
    ]
    mixed_all = jnp.concatenate(exchange_blocks(mixed_parts), axis=0)
    middle = hidden + dot(mixed_all, out_full, 0, 0) + out_bias[0]
    second, scaled_two, inverse_two = layer_norm(middle, norm_gain[1], norm_shift[1])
    second_rows = jnp.concatenate(gather_blocks(second.astype(BF16)), axis=0)

    upper = dot(second_rows, up_full, 1, 0) + up_bias
    active, slope = gelu_both(upper)
    active = active.astype(BF16)
    mlp_partial = dot(active, down_full, 1, 0).astype(BF16)
    grad_active = dot(grad_rows, down_full, 1, 1)
    grad_upper = (grad_active * slope).astype(BF16)
    second_partial = dot(grad_upper, up_full, 1, 1).astype(BF16)
    grad_second = scatter_blocks(rows_of(second_partial, tensor_size))
    mlp_sum = scatter_blocks(rows_of(mlp_partial, tensor_size))
    block_out = middle + mlp_sum + out_bias[1]

    grad_up_bias = jnp.sum(grad_upper.astype(F32), axis=0)
    grad_down = dot(active, grad_rows, 0, 0).astype(BF16)
    grad_up = dot(second_rows, grad_upper, 0, 0).astype(BF16)
    grad_up_weight = lax.psum_scatter(grad_up, "dp", scatter_dimension=0, tiled=True).astype(F32)
    grad_down_weight = lax.psum_scatter(
        grad_down, "dp", scatter_dimension=1, tiled=True
    ).astype(F32)

    grad_out = cotangent.astype(F32)
    grad_from_norm, gain_two, shift_two = norm_backward(
        grad_second, scaled_two, inverse_two, norm_gain[1]
    )
    grad_middle = grad_out + grad_from_norm
    grad_attn = grad_middle.astype(BF16)
    mixed_grads = dot(out_full, grad_attn, 1, 1).astype(BF16)
    grads_t = jnp.concatenate(exchange_blocks(rows_of(mixed_grads, tensor_size)), axis=1)
    out_partial = dot(mixed_all, grad_attn, 1, 0).astype(BF16)
    grad_out_mine = scatter_blocks(rows_of(out_partial, tensor_size)).astype(BF16)
    grad_out_weight = lax.psum_scatter(
        grad_out_mine, "dp", scatter_dimension=1, tiled=True
    ).astype(F32)

    early = jnp.stack(
        [gain_two, shift_two, jnp.sum(grad_middle, axis=0), jnp.sum(grad_out, axis=0)]
    )
    early = sum_over(early, ("dp", "tensor"))
    grad_up_bias = sum_over(grad_up_bias.reshape(-1, 128), ("dp",)).reshape(-1)

    query_low, key_low, value_low = attend_backward(
        place, slopes, queries_t, keys, values, grads_t, mixed_full, logs, local_rows, head_dim
    )
    normed_partial = (
        dot(query_low, qkv_full[0], 0, 1)
        + dot(key_low, qkv_full[1], 1, 1)
        + dot(value_low, qkv_full[2], 1, 1)
    ).astype(BF16)
    grad_normed = scatter_blocks(rows_of(normed_partial, tensor_size))
    grad_qkv_local = jnp.stack(
        [
            dot(normed_rows, query_low, 0, 1),
            dot(normed_rows, key_low, 0, 0),
            dot(normed_rows, value_low, 0, 0),
        ]
    ).astype(BF16)
    grad_qkv = lax.psum_scatter(grad_qkv_local, "dp", scatter_dimension=1, tiled=True).astype(F32)
    grad_from_first, gain_one, shift_one = norm_backward(
        grad_normed, scaled_one, inverse_one, norm_gain[0]
    )
    grad_in = grad_middle + grad_from_first
    late = sum_over(jnp.stack([gain_one, shift_one]), ("dp", "tensor"))
    grad_qv = jnp.stack(
        [jnp.sum(query_low.astype(F32), axis=1), jnp.sum(value_low.astype(F32), axis=0)]
    )
    grad_qv_bias = sum_over(grad_qv, ("dp",))
    return (
        block_out,
        grad_in,
        jnp.stack([late[0], early[0]]),
        jnp.stack([late[1], early[1]]),
        grad_qkv,
        grad_qv_bias,
        grad_out_weight,
        early[2:4],
        grad_up_weight,
        grad_up_bias,
        grad_down_weight,
    )


def solution(mesh):
    return jax.shard_map(
        body,
        mesh=mesh,
        in_specs=(
            P(("dp", "tensor"), None),
            P(),
            P(),
            P(None, "dp", "tensor"),
            P(None, "tensor"),
            P("tensor", "dp"),
            P(),
            P("dp", "tensor"),
            P("tensor"),
            P("tensor", "dp"),
            P(("dp", "tensor"), None),
        ),
        out_specs=(
            P(("dp", "tensor"), None),
            P(("dp", "tensor"), None),
            P(),
            P(),
            P(None, "dp", "tensor"),
            P(None, "tensor"),
            P("tensor", "dp"),
            P(),
            P("dp", "tensor"),
            P("tensor"),
            P("tensor", "dp"),
        ),
        check_vma=False,
    )
```

time: 1270 us -> 526 us (0.41)
  waiting for transfers between devices: 680 us -> 216 us
  matrix products: 305 us -> 84.1 us
  other arithmetic: 109 us -> 38.9 us
  Pallas kernels: 0 us -> 66.9 us
  blocking collectives: 98.1 us -> 32.1 us
  starting transfers between devices: 0.86 us -> 31.1 us
  local copies, waits for them, and re-layouts: 48.1 us -> 33.6 us
  loops' own time: 14.2 us -> 0 us
    reduce_scatter x7 -> x1, waiting for transfers between devices: 424 us -> 0.01 us  [body(): lax.psum_scatter(grad_up, 'dp', scatter_dimension=0, tiled=True).astype(F32)]
    all_gather x7 -> x3, waiting for transfers between devices: 239 us -> 0.04 us  [the longest x1 0.02 us: body(): qkv_full = lax.all_gather(qkv_weight, 'dp', axis=1, tiled=True)]
    dot_general x40 -> x18, matrix products: 305 us -> 84.1 us  [dot(): lax.dot_general(a, b, (((ca,), (cb,)), ((), ())), preferred_element_type=...]
    ppermute x0 -> x46, waiting for transfers between devices: none -> 142 us  [swap(): return lax.ppermute(value, axis, [(i, i ^ distance) for i in range(size)])]
    pallas_call x0 -> x2, Pallas kernels: none -> 66.9 us  [the longest x1 38.8 us: attend_backward(): pl.pallas_call(functools.partial(backward_kernel, scale=LOG2E / math.sqrt...]
    psum x2 -> x0, blocking collectives: 64.9 us -> none  [the longest x1 42.4 us: body(): lax.psum((gain_local, shift_local, bias_local), ('dp', 'tensor'))]
    convert_element_type x17 -> x11, other arithmetic: 58.2 us -> 13.9 us  [the longest x4 5.61 us: scatter_blocks(): return near + swap(far.astype(BF16), 'tensor', 2).astype(F32)]
    reduce_scatter x1, waiting for transfers between devices: 15.4 us -> 53.9 us  [body(): lax.psum_scatter(grad_qkv_local, 'dp', scatter_dimension=1, tiled=True)]
  transfers between devices with their start and end apart: 15 -> 53, of which waited for: 15 -> 20; matrix products, arithmetic and copies ran while one was open for 6% -> 29% of each run, Pallas kernels for 0% -> 13%
where the time goes in v1:
time: 526 us; the launch traced here: 517 us
  waiting for transfers between devices  216 us (41%)
  matrix products  84.1 us (16%)
  Pallas kernels  66.9 us (13%)
  other arithmetic  38.9 us (7%)
  local copies, waits for them, and re-layouts  33.6 us (6%)
  blocking collectives  32.1 us (6%)
  starting transfers between devices  31.1 us (6%)
  between operations  15.2 us (3%)
    ppermute x46, waiting for transfers between devices, swap(): return lax.ppermute(value, axis, [(i, i ^ distance) for i in range(size)])  142 us
    dot_general x18, matrix products, dot(): lax.dot_general(a, b, (((ca,), (cb,)), ((), ())), preferred_element_type=...  84.1 us
    reduce_scatter x1, waiting for transfers between devices, body(): lax.psum_scatter(grad_qkv_local, 'dp', scatter_dimension=1, tiled=True)  53.9 us
    pallas_call x1, Pallas kernels, attend_backward(): pl.pallas_call(functools.partial(backward_kernel, scale=LOG2E / math.sqrt...  38.8 us
    all_gather x1, blocking collectives, body(): out_mine = lax.all_gather(out_weight, 'dp', axis=1, tiled=True)  32.1 us
    ppermute x46, starting transfers between devices, swap(): return lax.ppermute(value, axis, [(i, i ^ distance) for i in range(size)])  30 us
    pallas_call x1, Pallas kernels, attend_forward(): pl.pallas_call(functools.partial(forward_kernel, scale=LOG2E / math.sqrt(...  28 us
    unnamed x88, local copies, waits for them, and re-layouts  22.7 us
  transfers between devices with their start and end apart: 53, of which 20 were waited for; matrix products, arithmetic and copies ran while one was open for 29% of the time, Pallas kernels for 13%

profile of v1, /device:TPU:0, one launch (start us, length us, event | category | flops | bytes accessed | tf_op | source)
XLA Modules:
  0.0 517.5 jit_solution(17225799216745663278)
XLA Ops:
  8.0 1.4 convert_reduce_fusion.1
  9.5 1.6 fusion.16
  12.7 1.7 fusion.10
  14.4 3.0 collective-permute-start.1
  17.4 23.3 %collective-permute-done.1 = bf16[512,1024]{1,0:T(8,128)(2,1)} collective-permute-done((bf16[512,1024]{1,0:T(8,128)(2,1)S(1)}, bf16[512,1024]{1,0:T(8,128)(2,1)}, u32[]{:S(2)}, u32[]{:S(2)}) %collective-permute-start.1) | collective-permute-done | bytes 1048608 | tf_op jit(solution)/shard_map/ppermute | solution.py:270
  40.7 32.1 %all_gather.13 = bf16[256,1024]{1,0:T(8,128)(2,1)} all-gather(bf16[256,128]{1,0:T(8,128)(2,1)S(1)} %copy-done.22), channel_id=1, replica_groups=mesh['dp'=8,'tensor'=4] {'dp'}, dimensions={1}, use_global_device_ids=true | all-gather | bytes 589824 | tf_op jit(solution)/shard_map/all_gather | solution.py:332
  72.8 1.6 collective-permute-start.7
  75.0 1.9 constant_dynamic-update-slice_fusion.3
  76.9 11.1 %collective-permute-done.7 = bf16[256,1024]{1,0:T(8,128)(2,1)} collective-permute-done((bf16[256,1024]{1,0:T(8,128)(2,1)}, bf16[256,1024]{1,0:T(8,128)(2,1)}, u32[]{:S(2)}, u32[]{:S(2)}) %collective-permute-start.7) | collective-permute-done | bytes 524320 | tf_op jit(solution)/shard_map/ppermute | solution.py:270
  88.1 3.4 convolution_convert_fusion.2.k_ref
  91.5 2.9 fusion.1.v_ref
  94.4 3.7 fusion.8.q_ref
  98.1 28.0 %attend_forward.1 = (bf16[256,2048]{1,0:T(8,128)(2,1)S(1)}, f32[256,2048]{1,0:T(8,128)}, f32[2,2,2048]{2,1,0:T(2,128)S(1)}) custom-call(s32[1]{0:T(128)} %bitcast.place, f32[4]{0:T(128)S(1)} %exponential_multiply_fusion.slope_ref, bf16[256,2048]{1,0:T(8,128)(2,1)S(1)} %fusion.8.q_ref, bf16[2048,256]{1,0:T(8,128)(2,1)S(1)} %convolution_convert_fusion.2.k_ref, ...), custom_call_target="tpu_custom_call" | custom-call | flops 20000000000 | bytes 8388608 | tf_op jit(solution)/shard_map/attend_forward/pallas_call | solution.py:196
  126.3 1.8 collective-permute-start.5
  131.7 3.0 collective-permute-done.5
  134.7 5.9 %collective-permute-done.4 = bf16[256,512]{1,0:T(8,128)(2,1)S(1)} collective-permute-done((bf16[256,512]{1,0:T(8,128)(2,1)S(1)}, bf16[256,512]{1,0:T(8,128)(2,1)S(1)}, u32[]{:S(2)}, u32[]{:S(2)}) %collective-permute-start.4) | collective-permute-done | bytes 262176 | tf_op jit(solution)/shard_map/ppermute | solution.py:270
  144.6 1.6 collective-permute-start.10
  147.2 22.4 %collective-permute-done.10 = bf16[512,1024]{1,0:T(8,128)(2,1)} collective-permute-done((bf16[512,1024]{1,0:T(8,128)(2,1)}, bf16[512,1024]{1,0:T(8,128)(2,1)}, u32[]{:S(2)}, u32[]{:S(2)}) %collective-permute-start.10) | collective-permute-done | bytes 1048608 | tf_op jit(solution)/shard_map/ppermute | solution.py:270
  170.6 2.3 constant_dynamic-update-slice_fusion.6
  172.9 2.3 constant_dynamic-update-slice_fusion.5
  176.3 8.1 %fusion.21 = f32[2048,1024]{1,0:T(8,128)S(1)} fusion(bf16[1024,1024]{1,0:T(8,128)(2,1)} %all-gather.6.cloned.1.call-done, bf16[512,1024]{1,0:T(8,128)(2,1)} %collective-permute-done.11, bf16[512,1024]{1,0:T(8,128)(2,1)} %collective-permute-done.10, bf16[512,1024]{1,0:T(8,128)(2,1)} %collective-permute-done.9, bf16[512,1024]{1,0:T(8,128)(2,1)} %add_convert_fusion.4), kind=kOutput, calls=%fused_computation.66 | convolution fusion | flops 4311744512 | bytes 14680064 | tf_op jit(solution)/shard_map/dot_general | solution.py:304
  184.4 3.3 copy-done.38
  187.7 8.3 %convolution_convert_fusion.3 = bf16[1024,1024]{1,0:T(8,128)(2,1)} fusion(bf16[2048,1024]{1,0:T(8,128)(2,1)} %constant_dynamic-update-slice_fusion.4, f32[2048,1024]{1,0:T(8,128)S(1)} %fusion.21, f32[1024]{0:T(1024)S(1)} %copy-done.37), kind=kOutput, calls=%fused_computation.49 | convolution fusion | flops 4316987392 | bytes 14684160 | tf_op jit(solution)/shard_map/dot_general | solution.py:304
  196.0 3.9 copy.30
  200.1 13.1 %convert_reduce_fusion = (f32[1024]{0:T(1024)S(1)}, bf16[2048,1024]{1,0:T(8,128)(2,1)S(1)}) fusion(f32[2048,1024]{1,0:T(8,128)} %copy-done.38, f32[1024]{0:T(1024)S(1)} %copy-done.37, bf16[2048,1024]{1,0:T(8,128)(2,1)} %constant_dynamic-update-slice_fusion.4, bf16[1024,1024]{1,0:T(8,128)(2,1)} %all-gather.8.cloned.1.call-done), kind=kOutput, calls=%fused_computation | convolution fusion | flops 4339006464 | bytes 18882560 | tf_op jit(solution)/shard_map/dot_general | solution.py:304
  213.2 5.1 convolution_convert_fusion
  219.9 1.6 copy-done.30
  221.5 9.2 %convolution_convert_fusion.1 = bf16[2048,1024]{1,0:T(8,128)(2,1)S(1)} fusion(bf16[1024,1024]{1,0:T(8,128)(2,1)S(1)} %copy-done.30, f32[2048,1024]{1,0:T(8,128)} %copy-done.38, f32[1024]{0:T(1024)S(1)} %copy-done.37), kind=kOutput, calls=%fused_computation.9 | convolution fusion | flops 4318035968 | bytes 14684160 | tf_op jit(solution)/shard_map/dot_general | solution.py:304
  233.2 2.9 collective-permute-done.43
  236.8 1.4 add_convert_fusion.2
  238.2 1.6 collective-permute-start.20
  241.6 8.2 %convolution_convert_fusion.4 = bf16[1024,1024]{1,0:T(8,128)(2,1)} fusion(bf16[2048,1024]{1,0:T(8,128)(2,1)S(1)} %get-tuple-element.66, bf16[512,1024]{1,0:T(8,128)(2,1)} %collective-permute-done.11, bf16[512,1024]{1,0:T(8,128)(2,1)} %collective-permute-done.10, bf16[512,1024]{1,0:T(8,128)(2,1)} %collective-permute-done.9, ...), kind=kOutput, calls=%fused_computation.50 | convolution fusion | flops 4312793088 | bytes 10485760 | tf_op jit(solution)/shard_map/dot_general | solution.py:304
  250.9 13.7 %collective-permute-done.20 = bf16[512,1024]{1,0:T(8,128)(2,1)} collective-permute-done((bf16[512,1024]{1,0:T(8,128)(2,1)}, bf16[512,1024]{1,0:T(8,128)(2,1)}, u32[]{:S(2)}, u32[]{:S(2)}) %collective-permute-start.20) | collective-permute-done | bytes 1048608 | tf_op jit(solution)/shard_map/ppermute | solution.py:270
  264.6 3.7 multiply_reduce_fusion
  268.3 16.3 %collective-permute-done.14 = bf16[512,1024]{1,0:T(8,128)(2,1)} collective-permute-done((bf16[512,1024]{1,0:T(8,128)(2,1)}, bf16[512,1024]{1,0:T(8,128)(2,1)}, u32[]{:S(2)}, u32[]{:S(2)}) %collective-permute-start.14) | collective-permute-done | bytes 1048608 | tf_op jit(solution)/shard_map/ppermute | solution.py:270
  284.7 4.8 fusion.35
  291.4 1.9 collective-permute-done.32
  293.3 1.4 collective-permute-start.33
  294.9 1.7 collective-permute-start.22
  299.5 2.4 collective-permute-done.34
  303.7 5.4 %collective-permute-done.22 = bf16[256,512]{1,0:T(8,128)(2,1)S(1)} collective-permute-done((bf16[256,512]{1,0:T(8,128)(2,1)S(1)}, bf16[256,512]{1,0:T(8,128)(2,1)S(1)}, u32[]{:S(2)}, u32[]{:S(2)}) %collective-permute-start.22) | collective-permute-done | bytes 262176 | tf_op jit(solution)/shard_map/ppermute | solution.py:270
  310.3 38.8 %attend_backward.1 = (bf16[256,2048]{1,0:T(8,128)(2,1)S(1)}, bf16[2048,256]{1,0:T(8,128)(2,1)S(1)}, bf16[2048,256]{1,0:T(8,128)(2,1)S(1)}) custom-call(s32[1]{0:T(128)} %bitcast.place, f32[4]{0:T(128)S(1)} %exponential_multiply_fusion.slope_ref, bf16[256,2048]{1,0:T(8,128)(2,1)S(1)} %fusion.8.q_ref, bf16[2048,256]{1,0:T(8,128)(2,1)S(1)} %convolution_convert_fusion.2.k_ref, ...), custom_call_target="tpu_custom_call" | custom-call | flops 40000000000 | bytes 12582912 | tf_op jit(solution)/shard_map/attend_backward/pallas_call | solution.py:232
  349.1 2.5 fusion.24
  352.9 3.6 add_convert_fusion
  356.5 3.1 fusion.36
  360.3 3.3 fusion.19
  363.8 1.9 collective-permute-start.42
  365.8 4.0 fusion.20
  370.0 8.3 %collective-permute-done.42 = bf16[256,1024]{1,0:T(8,128)(2,1)S(1)} collective-permute-done((bf16[256,1024]{1,0:T(8,128)(2,1)S(1)}, bf16[256,1024]{1,0:T(8,128)(2,1)S(1)}, u32[]{:S(2)}, u32[]{:S(2)}) %collective-permute-start.42) | collective-permute-done | bytes 524320 | tf_op jit(solution)/shard_map/ppermute | solution.py:270
  380.0 2.6 add_convert_fusion.1
  382.6 1.7 collective-permute-start.26
  384.4 3.5 fusion.18
  388.0 1.4 pad_maximum_fusion.2
  390.8 17.7 %collective-permute-done.26 = bf16[512,1024]{1,0:T(8,128)(2,1)} collective-permute-done((bf16[512,1024]{1,0:T(8,128)(2,1)}, bf16[512,1024]{1,0:T(8,128)(2,1)}, u32[]{:S(2)}, u32[]{:S(2)}) %collective-permute-start.26) | collective-permute-done | bytes 1048608 | tf_op jit(solution)/shard_map/ppermute | solution.py:270
  408.5 3.1 fusion.15
  413.1 2.3 collective-permute-done.27
  419.3 1.8 convert_element_type.200
  421.1 19.2 %reduce-scatter.13.cloned.1.call-done = bf16[128,256]{1,0:T(8,128)(2,1)} async-done(((bf16[1024,256]{1,0:T(8,128)(2,1)}), bf16[128,256]{1,0:T(8,128)(2,1)}) %reduce-scatter.13.cloned.1.call-update) | async-done | bytes 65552
  442.0 1.5 collective-permute-start.29
  443.5 3.1 collective-permute-done.29
  447.8 1.5 collective-permute-start.31
  449.3 4.3 fusion.14
  454.8 53.9 %reduce-scatter.9.cloned.1.call-done = bf16[3,128,256]{2,1,0:T(8,128)(2,1)} async-done(((bf16[3,1024,256]{2,1,0:T(8,128)(2,1)}), bf16[3,128,256]{2,1,0:T(8,128)(2,1)}) %reduce-scatter.9.cloned.1.call-update) | async-done | bytes 196624 | tf_op jit(solution)/shard_map/reduce_scatter | solution.py:411
  508.7 1.7 convert_element_type.187
  (224 shorter events, 44.3 us)
Async XLA Ops:
  7.2 33.5 %copy-start.22 = (bf16[256,128]{1,0:T(8,128)(2,1)S(1)}, bf16[256,128]{1,0:T(8,128)(2,1)}, u32[]{:S(2)}) copy-start(bf16[256,128]{1,0:T(8,128)(2,1)} %param.16) | copy-start | bytes 196612
  7.2 67.3 %copy-start.9 = (bf16[512,1024]{1,0:T(8,128)(2,1)S(1)}, bf16[512,1024]{1,0:T(8,128)(2,1)}, u32[]{:S(2)}) copy-start(bf16[512,1024]{1,0:T(8,128)(2,1)} %param.21) | copy-start | bytes 3145732
  7.2 69.6 %copy-start.28 = (f32[2,256]{1,0:T(2,128)S(1)}, f32[2,256]{1,0:T(2,128)}, u32[]{:S(2)}) copy-start(f32[2,256]{1,0:T(2,128)} %param.15) | copy-start | bytes 6148
  7.2 69.6 %copy-start.27 = (f32[2,1024]{1,0:T(2,128)S(1)}, f32[2,1024]{1,0:T(2,128)}, u32[]{:S(2)}) copy-start(f32[2,1024]{1,0:T(2,128)} %param.17) | copy-start | bytes 24580
  7.2 80.8 %all-gather.4.cloned.1.call-start = ((), (), s32[]{:S(2)}) async-start(), calls=%async_computation.4 | async-start | bytes 1769472 | tf_op jit(solution)/shard_map/all_gather | solution.py:331
  8.0 168.3 %all-gather.6.cloned.1.call-start = ((), (), s32[]{:S(2)}) async-start(), calls=%async_computation.5 | async-start | bytes 2359296 | tf_op jit(solution)/shard_map/all_gather | solution.py:333
  9.4 78.6 %copy-start.23 = (f32[512]{0:T(512)}, f32[512]{0:T(512)S(1)}, u32[]{:S(2)}) copy-start(f32[512]{0:T(512)S(1)} %broadcast_multiply_fusion.5) | copy-start | bytes 6148
  11.1 76.9 %copy-start.25 = (f32[512]{0:T(512)}, f32[512]{0:T(512)S(1)}, u32[]{:S(2)}) copy-start(f32[512]{0:T(512)S(1)} %add_rsqrt_fusion.1) | copy-start | bytes 6148
  11.9 63.0 %copy-start.20 = (f32[1,1024]{1,0:T(1,128)}, f32[1,1024]{1,0:T(1,128)S(1)}, u32[]{:S(2)}) copy-start(f32[1,1024]{1,0:T(1,128)S(1)} %get-tuple-element.58) | copy-start | bytes 12292
  14.4 77.1 %copy-start.14 = (bf16[512,1024]{1,0:T(8,128)(2,1)}, bf16[512,1024]{1,0:T(8,128)(2,1)S(1)}, u32[]{:S(2)}) copy-start(bf16[512,1024]{1,0:T(8,128)(2,1)S(1)} %fusion.10) | copy-start | bytes 3145732
  14.4 26.3 %collective-permute-start.1 = (bf16[512,1024]{1,0:T(8,128)(2,1)S(1)}, bf16[512,1024]{1,0:T(8,128)(2,1)}, u32[]{:S(2)}, u32[]{:S(2)}) collective-permute-start(bf16[512,1024]{1,0:T(8,128)(2,1)S(1)} %fusion.10), channel_id=1, source_target_pairs={{0,2},{1,3},{2,0},{3,1},{4,6},{5,7},{6,4},{7,5},{8,10},{9,11},{10,... | collective-permute-start | bytes 3145736 | tf_op jit(solution)/shard_map/ppermute | solution.py:270
  17.4 70.6 %collective-permute-start = (bf16[512,1024]{1,0:T(8,128)(2,1)S(1)}, bf16[512,1024]{1,0:T(8,128)(2,1)}, u32[]{:S(2)}, u32[]{:S(2)}) collective-permute-start(bf16[512,1024]{1,0:T(8,128)(2,1)S(1)} %fusion.10), channel_id=1, source_target_pairs={{0,1},{1,0},{2,3},{3,2},{4,5},{5,4},{6,7},{7,6},{8,9},{9,8},{10,11... | collective-permute-start | bytes 3145736 | tf_op jit(solution)/shard_map/ppermute | solution.py:270
  40.7 47.3 %collective-permute-start.2 = (bf16[512,1024]{1,0:T(8,128)(2,1)}, bf16[512,1024]{1,0:T(8,128)(2,1)}, u32[]{:S(2)}, u32[]{:S(2)}) collective-permute-start(bf16[512,1024]{1,0:T(8,128)(2,1)} %collective-permute-done.1), channel_id=1, source_target_pairs={{0,1},{1,0},{2,3},{3,2},{4,5},{5,4},{6,7},{7,6},{8,9},{9,8},{10,11... | collective-permute-start | bytes 3145736 | tf_op jit(solution)/shard_map/ppermute | solution.py:270
  72.8 15.2 %collective-permute-start.7 = (bf16[256,1024]{1,0:T(8,128)(2,1)}, bf16[256,1024]{1,0:T(8,128)(2,1)}, u32[]{:S(2)}, u32[]{:S(2)}) collective-permute-start(bf16[256,1024]{1,0:T(8,128)(2,1)} %all_gather.13), channel_id=1, source_target_pairs={{0,2},{1,3},{2,0},{3,1},{4,6},{5,7},{6,4},{7,5},{8,10},{9,11},{10,... | collective-permute-start | bytes 1572872 | tf_op jit(solution)/shard_map/ppermute | solution.py:270
  74.4 54.0 %collective-permute-start.6 = (bf16[256,1024]{1,0:T(8,128)(2,1)}, bf16[256,1024]{1,0:T(8,128)(2,1)}, u32[]{:S(2)}, u32[]{:S(2)}) collective-permute-start(bf16[256,1024]{1,0:T(8,128)(2,1)} %all_gather.13), channel_id=1, source_target_pairs={{0,1},{1,0},{2,3},{3,2},{4,5},{5,4},{6,7},{7,6},{8,9},{9,8},{10,11... | collective-permute-start | bytes 1572872 | tf_op jit(solution)/shard_map/ppermute | solution.py:270
  74.4 72.0 %collective-permute-start.16 = (bf16[512,1024]{1,0:T(8,128)(2,1)S(1)}, bf16[512,1024]{1,0:T(8,128)(2,1)}, u32[]{:S(2)}, u32[]{:S(2)}) collective-permute-start(bf16[512,1024]{1,0:T(8,128)(2,1)S(1)} %copy-done.9), channel_id=1, source_target_pairs={{0,2},{1,3},{2,0},{3,1},{4,6},{5,7},{6,4},{7,5},{8,10},{9,11},{10,... | collective-permute-start | bytes 3145736 | tf_op jit(solution)/shard_map/ppermute | solution.py:270
  74.9 125.2 %all-gather.8.cloned.1.call-start = ((), (), s32[]{:S(2)}) async-start(), calls=%async_computation.6 | async-start | bytes 2359296 | tf_op jit(solution)/shard_map/all_gather | solution.py:334
  88.0 42.6 %collective-permute-start.8 = (bf16[256,1024]{1,0:T(8,128)(2,1)}, bf16[256,1024]{1,0:T(8,128)(2,1)}, u32[]{:S(2)}, u32[]{:S(2)}) collective-permute-start(bf16[256,1024]{1,0:T(8,128)(2,1)} %collective-permute-done.7), channel_id=1, source_target_pairs={{0,1},{1,0},{2,3},{3,2},{4,5},{5,4},{6,7},{7,6},{8,9},{9,8},{10,11... | collective-permute-start | bytes 1572872 | tf_op jit(solution)/shard_map/ppermute | solution.py:270
  98.1 30.3 %copy-start.17 = (bf16[1024,1024]{1,0:T(8,128)(2,1)S(1)}, bf16[1024,1024]{1,0:T(8,128)(2,1)}, u32[]{:S(2)}) copy-start(bf16[1024,1024]{1,0:T(8,128)(2,1)} %constant_dynamic-update-slice_fusion.3) | copy-start | bytes 6291460
  126.3 8.4 %collective-permute-start.5 = (bf16[256,512]{1,0:T(8,128)(2,1)S(1)}, bf16[256,512]{1,0:T(8,128)(2,1)S(1)}, u32[]{:S(2)}, u32[]{:S(2)}) collective-permute-start(bf16[256,512]{1,0:T(8,128)(2,1)S(1)} %get-tuple-element.48), channel_id=1, source_target_pairs={{0,3},{1,2},{2,1},{3,0},{4,7},{5,6},{6,5},{7,4},{8,11},{9,10},{10,... | collective-permute-start | bytes 786440 | tf_op jit(solution)/shard_map/ppermute | solution.py:270
  128.0 12.5 %collective-permute-start.4 = (bf16[256,512]{1,0:T(8,128)(2,1)S(1)}, bf16[256,512]{1,0:T(8,128)(2,1)S(1)}, u32[]{:S(2)}, u32[]{:S(2)}) collective-permute-start(bf16[256,512]{1,0:T(8,128)(2,1)S(1)} %get-tuple-element.49), channel_id=1, source_target_pairs={{0,2},{1,3},{2,0},{3,1},{4,6},{5,7},{6,4},{7,5},{8,10},{9,11},{10,... | collective-permute-start | bytes 786440 | tf_op jit(solution)/shard_map/ppermute | solution.py:270
  128.5 12.1 %collective-permute-start.3 = (bf16[256,512]{1,0:T(8,128)(2,1)S(1)}, bf16[256,512]{1,0:T(8,128)(2,1)S(1)}, u32[]{:S(2)}, u32[]{:S(2)}) collective-permute-start(bf16[256,512]{1,0:T(8,128)(2,1)S(1)} %get-tuple-element.50), channel_id=1, source_target_pairs={{0,1},{1,0},{2,3},{3,2},{4,5},{5,4},{6,7},{7,6},{8,9},{9,8},{10,11... | collective-permute-start | bytes 786440 | tf_op jit(solution)/shard_map/ppermute | solution.py:270
  144.6 24.9 %collective-permute-start.10 = (bf16[512,1024]{1,0:T(8,128)(2,1)}, bf16[512,1024]{1,0:T(8,128)(2,1)}, u32[]{:S(2)}, u32[]{:S(2)}) collective-permute-start(bf16[512,1024]{1,0:T(8,128)(2,1)} %add_convert_fusion.4), channel_id=1, source_target_pairs={{0,2},{1,3},{2,0},{3,1},{4,6},{5,7},{6,4},{7,5},{8,10},{9,11},{10,... | collective-permute-start | bytes 3145736 | tf_op jit(solution)/shard_map/ppermute | solution.py:270
  146.2 24.3 %collective-permute-start.15 = (bf16[512,1024]{1,0:T(8,128)(2,1)S(1)}, bf16[512,1024]{1,0:T(8,128)(2,1)}, u32[]{:S(2)}, u32[]{:S(2)}) collective-permute-start(bf16[512,1024]{1,0:T(8,128)(2,1)S(1)} %copy-done.9), channel_id=1, source_target_pairs={{0,1},{1,0},{2,3},{3,2},{4,5},{5,4},{6,7},{7,6},{8,9},{9,8},{10,11... | collective-permute-start | bytes 3145736 | tf_op jit(solution)/shard_map/ppermute | solution.py:270
  146.3 271.1 %reduce-scatter.15.cloned.1.call-start = ((), (), s32[]{:S(2)}) async-start(), calls=%async_computation.10 | async-start | bytes 2359296
  146.5 28.7 %collective-permute-start.17 = (bf16[512,1024]{1,0:T(8,128)(2,1)}, bf16[512,1024]{1,0:T(8,128)(2,1)S(1)}, u32[]{:S(2)}, u32[]{:S(2)}) collective-permute-start(bf16[512,1024]{1,0:T(8,128)(2,1)} %collective-permute-done.16), channel_id=1, source_target_pairs={{0,1},{1,0},{2,3},{3,2},{4,5},{5,4},{6,7},{7,6},{8,9},{9,8},{10,11... | collective-permute-start | bytes 3145736 | tf_op jit(solution)/shard_map/ppermute | solution.py:270
  147.1 29.2 %collective-permute-start.9 = (bf16[512,1024]{1,0:T(8,128)(2,1)}, bf16[512,1024]{1,0:T(8,128)(2,1)}, u32[]{:S(2)}, u32[]{:S(2)}) collective-permute-start(bf16[512,1024]{1,0:T(8,128)(2,1)} %add_convert_fusion.4), channel_id=1, source_target_pairs={{0,1},{1,0},{2,3},{3,2},{4,5},{5,4},{6,7},{7,6},{8,9},{9,8},{10,11... | collective-permute-start | bytes 3145736 | tf_op jit(solution)/shard_map/ppermute | solution.py:270
  169.5 6.8 %collective-permute-start.11 = (bf16[512,1024]{1,0:T(8,128)(2,1)}, bf16[512,1024]{1,0:T(8,128)(2,1)}, u32[]{:S(2)}, u32[]{:S(2)}) collective-permute-start(bf16[512,1024]{1,0:T(8,128)(2,1)} %collective-permute-done.10), channel_id=1, source_target_pairs={{0,1},{1,0},{2,3},{3,2},{4,5},{5,4},{6,7},{7,6},{8,9},{9,8},{10,11... | collective-permute-start | bytes 3145736 | tf_op jit(solution)/shard_map/ppermute | solution.py:270
  200.0 219.3 %reduce-scatter.11.cloned.1.call-start = ((), (), s32[]{:S(2)}) async-start(), calls=%async_computation.8 | async-start | bytes 2359296 | tf_op jit(solution)/shard_map/reduce_scatter | solution.py:370
  219.4 17.4 %collective-permute-start.19 = (bf16[512,1024]{1,0:T(8,128)(2,1)S(1)}, bf16[512,1024]{1,0:T(8,128)(2,1)S(1)}, u32[]{:S(2)}, u32[]{:S(2)}) collective-permute-start(bf16[512,1024]{1,0:T(8,128)(2,1)S(1)} %get-tuple-element.36), channel_id=1, source_target_pairs={{0,1},{1,0},{2,3},{3,2},{4,5},{5,4},{6,7},{7,6},{8,9},{9,8},{10,11... | collective-permute-start | bytes 3145736 | tf_op jit(solution)/shard_map/ppermute | solution.py:270
  232.0 7.8 %collective-permute-start.13 = (bf16[512,1024]{1,0:T(8,128)(2,1)S(1)}, bf16[512,1024]{1,0:T(8,128)(2,1)S(1)}, u32[]{:S(2)}, u32[]{:S(2)}) collective-permute-start(bf16[512,1024]{1,0:T(8,128)(2,1)S(1)} %get-tuple-element.38), channel_id=1, source_target_pairs={{0,1},{1,0},{2,3},{3,2},{4,5},{5,4},{6,7},{7,6},{8,9},{9,8},{10,11... | collective-permute-start | bytes 3145736 | tf_op jit(solution)/shard_map/ppermute | solution.py:270
  232.5 3.6 collective-permute-start.43
  232.7 18.2 %collective-permute-start.18 = (bf16[512,1024]{1,0:T(8,128)(2,1)}, bf16[512,1024]{1,0:T(8,128)(2,1)}, u32[]{:S(2)}, u32[]{:S(2)}) collective-permute-start(bf16[512,1024]{1,0:T(8,128)(2,1)} %get-tuple-element.35), channel_id=1, source_target_pairs={{0,1},{1,0},{2,3},{3,2},{4,5},{5,4},{6,7},{7,6},{8,9},{9,8},{10,11... | collective-permute-start | bytes 3145736 | tf_op jit(solution)/shard_map/ppermute | solution.py:270
  232.7 35.6 %collective-permute-start.12 = (bf16[512,1024]{1,0:T(8,128)(2,1)}, bf16[512,1024]{1,0:T(8,128)(2,1)}, u32[]{:S(2)}, u32[]{:S(2)}) collective-permute-start(bf16[512,1024]{1,0:T(8,128)(2,1)} %get-tuple-element.37), channel_id=1, source_target_pairs={{0,1},{1,0},{2,3},{3,2},{4,5},{5,4},{6,7},{7,6},{8,9},{9,8},{10,11... | collective-permute-start | bytes 3145736 | tf_op jit(solution)/shard_map/ppermute | solution.py:270
  236.1 14.2 %collective-permute-start.44 = (f32[8,128]{1,0:T(8,128)S(1)}, f32[8,128]{1,0:T(8,128)S(1)}, u32[]{:S(2)}, u32[]{:S(2)}) collective-permute-start(f32[8,128]{1,0:T(8,128)S(1)} %bitcast_add_fusion), channel_id=1, source_target_pairs={{0,8},{4,12},{8,0},{12,4},{16,24},{20,28},{24,16},{28,20},{1,9},{5... | collective-permute-start | bytes 12296 | tf_op jit(solution)/shard_map/ppermute | solution.py:270
  238.2 26.4 %collective-permute-start.20 = (bf16[512,1024]{1,0:T(8,128)(2,1)}, bf16[512,1024]{1,0:T(8,128)(2,1)}, u32[]{:S(2)}, u32[]{:S(2)}) collective-permute-start(bf16[512,1024]{1,0:T(8,128)(2,1)} %add_convert_fusion.2), channel_id=1, source_target_pairs={{0,2},{1,3},{2,0},{3,1},{4,6},{5,7},{6,4},{7,5},{8,10},{9,11},{10,... | collective-permute-start | bytes 3145736 | tf_op jit(solution)/shard_map/ppermute | solution.py:270
  241.2 43.4 %collective-permute-start.14 = (bf16[512,1024]{1,0:T(8,128)(2,1)}, bf16[512,1024]{1,0:T(8,128)(2,1)}, u32[]{:S(2)}, u32[]{:S(2)}) collective-permute-start(bf16[512,1024]{1,0:T(8,128)(2,1)} %add_convert_fusion.3), channel_id=1, source_target_pairs={{0,2},{1,3},{2,0},{3,1},{4,6},{5,7},{6,4},{7,5},{8,10},{9,11},{10,... | collective-permute-start | bytes 3145736 | tf_op jit(solution)/shard_map/ppermute | solution.py:270
  249.9 190.4 %reduce-scatter.13.cloned.1.call-start = ((), (), s32[]{:S(2)}) async-start(), calls=%async_computation.9 | async-start | bytes 589824
  250.3 34.3 %copy-start.2 = (f32[512,1024]{1,0:T(8,128)S(1)}, f32[512,1024]{1,0:T(8,128)}, u32[]{:S(2)}) copy-start(f32[512,1024]{1,0:T(8,128)} %copy-done.1) | copy-start | bytes 6291460
  250.4 139.0 %collective-permute-start.45 = (f32[8,128]{1,0:T(8,128)S(1)}, f32[8,128]{1,0:T(8,128)S(1)}, u32[]{:S(2)}, u32[]{:S(2)}) collective-permute-start(f32[8,128]{1,0:T(8,128)S(1)} %fusion.65), channel_id=1, source_target_pairs={{0,16},{4,20},{8,24},{12,28},{16,0},{20,4},{24,8},{28,12},{1,17},{... | collective-permute-start | bytes 12296 | tf_op jit(solution)/shard_map/ppermute | solution.py:270
  289.5 3.8 collective-permute-start.32
  293.3 3.9 collective-permute-start.33
  294.8 8.5 %collective-permute-start.23 = (bf16[256,512]{1,0:T(8,128)(2,1)S(1)}, bf16[256,512]{1,0:T(8,128)(2,1)S(1)}, u32[]{:S(2)}, u32[]{:S(2)}) collective-permute-start(bf16[256,512]{1,0:T(8,128)(2,1)S(1)} %get-tuple-element.44), channel_id=1, source_target_pairs={{0,3},{1,2},{2,1},{3,0},{4,7},{5,6},{6,5},{7,4},{8,11},{9,10},{10,... | collective-permute-start | bytes 786440 | tf_op jit(solution)/shard_map/ppermute | solution.py:270
  294.9 14.2 %collective-permute-start.22 = (bf16[256,512]{1,0:T(8,128)(2,1)S(1)}, bf16[256,512]{1,0:T(8,128)(2,1)S(1)}, u32[]{:S(2)}, u32[]{:S(2)}) collective-permute-start(bf16[256,512]{1,0:T(8,128)(2,1)S(1)} %get-tuple-element.45), channel_id=1, source_target_pairs={{0,2},{1,3},{2,0},{3,1},{4,6},{5,7},{6,4},{7,5},{8,10},{9,11},{10,... | collective-permute-start | bytes 786440 | tf_op jit(solution)/shard_map/ppermute | solution.py:270
  296.6 12.5 %collective-permute-start.21 = (bf16[256,512]{1,0:T(8,128)(2,1)S(1)}, bf16[256,512]{1,0:T(8,128)(2,1)S(1)}, u32[]{:S(2)}, u32[]{:S(2)}) collective-permute-start(bf16[256,512]{1,0:T(8,128)(2,1)S(1)} %get-tuple-element.46), channel_id=1, source_target_pairs={{0,1},{1,0},{2,3},{3,2},{4,5},{5,4},{6,7},{7,6},{8,9},{9,8},{10,11... | collective-permute-start | bytes 786440 | tf_op jit(solution)/shard_map/ppermute | solution.py:270
  297.2 4.7 collective-permute-start.34
  301.9 1.2 collective-permute-start.35
  303.1 66.6 %collective-permute-start.40 = (bf16[256,1024]{1,0:T(8,128)(2,1)S(1)}, bf16[256,1024]{1,0:T(8,128)(2,1)S(1)}, u32[]{:S(2)}, u32[]{:S(2)}) collective-permute-start(bf16[256,1024]{1,0:T(8,128)(2,1)S(1)} %get-tuple-element.39), channel_id=1, source_target_pairs={{0,1},{1,0},{2,3},{3,2},{4,5},{5,4},{6,7},{7,6},{8,9},{9,8},{10,11... | collective-permute-start | bytes 1572872 | tf_op jit(solution)/shard_map/ppermute | solution.py:270
  303.3 60.3 %collective-permute-start.41 = (bf16[256,1024]{1,0:T(8,128)(2,1)}, bf16[256,1024]{1,0:T(8,128)(2,1)S(1)}, u32[]{:S(2)}, u32[]{:S(2)}) collective-permute-start(bf16[256,1024]{1,0:T(8,128)(2,1)} %get-tuple-element.40), channel_id=1, source_target_pairs={{0,1},{1,0},{2,3},{3,2},{4,5},{5,4},{6,7},{7,6},{8,9},{9,8},{10,11... | collective-permute-start | bytes 1572872 | tf_op jit(solution)/shard_map/ppermute | solution.py:270
  309.1 80.9 %collective-permute-start.36 = (f32[4,1024]{1,0:T(4,128)S(1)}, f32[4,1024]{1,0:T(4,128)S(1)}, u32[]{:S(2)}, u32[]{:S(2)}) collective-permute-start(f32[4,1024]{1,0:T(4,128)S(1)} %add.268), channel_id=1, source_target_pairs={{0,2},{1,3},{2,0},{3,1},{4,6},{5,7},{6,4},{7,5},{8,10},{9,11},{10,... | collective-permute-start | bytes 49160 | tf_op jit(solution)/shard_map/ppermute | solution.py:270
  359.6 20.4 %collective-permute-start.25 = (bf16[512,1024]{1,0:T(8,128)(2,1)}, bf16[512,1024]{1,0:T(8,128)(2,1)S(1)}, u32[]{:S(2)}, u32[]{:S(2)}) collective-permute-start(bf16[512,1024]{1,0:T(8,128)(2,1)} %get-tuple-element.34), channel_id=1, source_target_pairs={{0,1},{1,0},{2,3},{3,2},{4,5},{5,4},{6,7},{7,6},{8,9},{9,8},{10,11... | collective-permute-start | bytes 3145736 | tf_op jit(solution)/shard_map/ppermute | solution.py:270
  363.8 14.5 %collective-permute-start.42 = (bf16[256,1024]{1,0:T(8,128)(2,1)S(1)}, bf16[256,1024]{1,0:T(8,128)(2,1)S(1)}, u32[]{:S(2)}, u32[]{:S(2)}) collective-permute-start(bf16[256,1024]{1,0:T(8,128)(2,1)S(1)} %add_convert_fusion.6), channel_id=1, source_target_pairs={{0,2},{1,3},{2,0},{3,1},{4,6},{5,7},{6,4},{7,5},{8,10},{9,11},{10,... | collective-permute-start | bytes 1572872 | tf_op jit(solution)/shard_map/ppermute | solution.py:270
  369.7 20.3 %collective-permute-start.37 = (f32[2,256]{1,0:T(2,128)S(1)}, f32[2,256]{1,0:T(2,128)S(1)}, u32[]{:S(2)}, u32[]{:S(2)}) collective-permute-start(f32[2,256]{1,0:T(2,128)S(1)} %pad_maximum_fusion.13), channel_id=1, source_target_pairs={{0,4},{4,0},{8,12},{12,8},{16,20},{20,16},{24,28},{28,24},{1,5},{5... | collective-permute-start | bytes 6152 | tf_op jit(solution)/shard_map/ppermute | solution.py:270
  378.4 12.4 %collective-permute-start.24 = (bf16[512,1024]{1,0:T(8,128)(2,1)}, bf16[512,1024]{1,0:T(8,128)(2,1)}, u32[]{:S(2)}, u32[]{:S(2)}) collective-permute-start(bf16[512,1024]{1,0:T(8,128)(2,1)} %get-tuple-element.33), channel_id=1, source_target_pairs={{0,1},{1,0},{2,3},{3,2},{4,5},{5,4},{6,7},{7,6},{8,9},{9,8},{10,11... | collective-permute-start | bytes 3145736 | tf_op jit(solution)/shard_map/ppermute | solution.py:270
  379.7 129.0 %reduce-scatter.9.cloned.1.call-start = ((), (), s32[]{:S(2)}) async-start(), calls=%async_computation.7 | async-start | bytes 1769472 | tf_op jit(solution)/shard_map/reduce_scatter | solution.py:411
  382.6 25.9 %collective-permute-start.26 = (bf16[512,1024]{1,0:T(8,128)(2,1)}, bf16[512,1024]{1,0:T(8,128)(2,1)}, u32[]{:S(2)}, u32[]{:S(2)}) collective-permute-start(bf16[512,1024]{1,0:T(8,128)(2,1)} %add_convert_fusion.1), channel_id=1, source_target_pairs={{0,2},{1,3},{2,0},{3,1},{4,6},{5,7},{6,4},{7,5},{8,10},{9,11},{10,... | collective-permute-start | bytes 3145736 | tf_op jit(solution)/shard_map/ppermute | solution.py:270
  389.4 59.9 %copy-start.6 = (f32[512,1024]{1,0:T(8,128)S(1)}, f32[512,1024]{1,0:T(8,128)}, u32[]{:S(2)}) copy-start(f32[512,1024]{1,0:T(8,128)} %copy-done.5) | copy-start | bytes 6291460
  390.0 22.0 %collective-permute-start.38 = (f32[2,256]{1,0:T(2,128)S(1)}, f32[2,256]{1,0:T(2,128)S(1)}, u32[]{:S(2)}, u32[]{:S(2)}) collective-permute-start(f32[2,256]{1,0:T(2,128)S(1)} %fusion.30), channel_id=1, source_target_pairs={{0,8},{4,12},{8,0},{12,4},{16,24},{20,28},{24,16},{28,20},{1,9},{5... | collective-permute-start | bytes 6152 | tf_op jit(solution)/shard_map/ppermute | solution.py:270
  411.6 3.7 collective-permute-start.27
  412.0 4.7 collective-permute-start.39
  415.4 26.6 %collective-permute-start.28 = (f32[2,1024]{1,0:T(2,128)S(1)}, f32[2,1024]{1,0:T(2,128)S(1)}, u32[]{:S(2)}, u32[]{:S(2)}) collective-permute-start(f32[2,1024]{1,0:T(2,128)S(1)} %fusion.31), channel_id=1, source_target_pairs={{0,8},{4,12},{8,0},{12,4},{16,24},{20,28},{24,16},{28,20},{1,9},{5... | collective-permute-start | bytes 24584 | tf_op jit(solution)/shard_map/ppermute | solution.py:270
  442.0 4.6 collective-permute-start.29
  446.6 1.2 collective-permute-start.30
  447.8 5.8 %collective-permute-start.31 = (f32[2,1024]{1,0:T(2,128)S(1)}, f32[2,1024]{1,0:T(2,128)S(1)}, u32[]{:S(2)}, u32[]{:S(2)}) collective-permute-start(f32[2,1024]{1,0:T(2,128)S(1)} %add.263), channel_id=1, source_target_pairs={{0,2},{1,3},{2,0},{3,1},{4,6},{5,7},{6,4},{7,5},{8,10},{9,11},{10,... | collective-permute-start | bytes 24584 | tf_op jit(solution)/shard_map/ppermute | solution.py:270
  (28 other events, 249.7 us)
Sparse Core Ops, SparseCore 0:
  10.2 48.0 all-gather.3
  75.0 46.9 all-gather.5
  146.4 47.5 all-gather.7
  200.1 65.4 reduce-scatter.14
  269.0 66.7 reduce-scatter.10
  379.8 60.4 reduce-scatter.12
  444.1 64.4 reduce-scatter.8

commit v2 on v1

v2 whole, which is shorter than its diff:
```python
import functools
import math

import jax
import jax.numpy as jnp
from jax import lax
from jax.experimental import pallas as pl
from jax.experimental.pallas import tpu as pltpu
from jax.sharding import PartitionSpec as P

HEADS = 16
LOG2E = 1.4426950408889634
NEG = -1e30
BF16 = jnp.bfloat16
F32 = jnp.float32


def normalise(values):
    average = jnp.mean(values, axis=-1, keepdims=True)
    centered = values - average
    inverse = lax.rsqrt(jnp.mean(centered * centered, axis=-1, keepdims=True) + 1e-05)
    return centered * inverse, inverse


def gelu_both(values):
    first = 0.7978845608
    square = values * values
    tangent = jnp.tanh(values * (first + (first * 0.044715) * square))
    half = 0.5 + 0.5 * tangent
    active = values * half
    slope = half + (values - values * (tangent * tangent)) * (
        0.5 * first + (1.5 * 0.044715 * first) * square
    )
    return active, slope


def first_norm_kernel(hidden, gain, shift, put_normed):
    scaled, _ = normalise(hidden().astype(F32))
    put_normed((scaled * gain()[0:1, :] + shift()[0:1, :]).astype(BF16))


def second_norm_kernel(hidden, attn, bias, gain, shift, put_middle, put_normed):
    middle = hidden().astype(F32) + attn() + bias()[0:1, :]
    put_middle(middle)
    scaled, _ = normalise(middle)
    put_normed((scaled * gain()[1:2, :] + shift()[1:2, :]).astype(BF16))


def back_of_norm(value, own, near, far, gain):
    scaled, inverse = normalise(value.astype(F32))
    gradient = own.astype(F32) + near.astype(F32) + far.astype(F32)
    grad_scaled = gradient * gain
    grad_mean = jnp.mean(grad_scaled, axis=-1, keepdims=True)
    grad_proj = jnp.mean(grad_scaled * scaled, axis=-1, keepdims=True)
    return inverse * (grad_scaled - grad_mean - scaled * grad_proj), gradient, scaled


def second_back_kernel(middle, above, own, near, far, gain, put_total, put_low, add_sums):
    change, gradient, scaled = back_of_norm(middle(), own(), near(), far(), gain()[1:2, :])
    grads = above().astype(F32)
    total = grads + change
    put_total(total)
    put_low(total.astype(BF16))
    columns = [gradient * scaled, gradient, total, grads]
    add_sums(jnp.concatenate([jnp.sum(c, axis=0, keepdims=True) for c in columns], axis=0))


def first_back_kernel(hidden, above, own, near, far, gain, put_total):
    change, _, _ = back_of_norm(hidden(), own(), near(), far(), gain()[0:1, :])
    put_total(above() + change)


def row_call(kernel, rows, width, arrays, outs, name, tile=128):
    tile = min(tile, rows // 2)
    half = rows // 2 // tile

    def specs(array):
        if isinstance(array, tuple):
            return [
                pl.BlockSpec((tile, width), lambda i: (jnp.minimum(i, half - 1), 0)),
                pl.BlockSpec((tile, width), lambda i: (jnp.maximum(i - half, 0), 0)),
            ]
        if array.shape[0] == rows:
            return [pl.BlockSpec((tile, width), lambda i: (i, 0))]
        return [pl.BlockSpec(array.shape, lambda i: (0, 0))]

    def flat(values):
        return [v for value in values for v in (value if isinstance(value, tuple) else (value,))]

    def run(*refs):
        step = pl.program_id(0)
        at = 0
        accesses = []
        for k, value in enumerate(arrays + outs):
            reads = k < len(arrays)
            if isinstance(value, tuple):
                one, two = refs[at : at + 2]
                at += 2
                if reads:
                    accesses.append(lambda a=one, b=two: jnp.where(step < half, a[...], b[...]))
                else:

                    def put(block, a=one, b=two):
                        @pl.when(step < half)
                        def _():
                            a[...] = block

                        @pl.when(step >= half)
                        def _():
                            b[...] = block

                    accesses.append(put)
                continue
            ref = refs[at]
            at += 1
            if reads:
                accesses.append(lambda a=ref: a[...])
            elif value.shape[0] == rows:

                def put(block, a=ref):
                    a[...] = block

                accesses.append(put)
            else:

                def add(block, a=ref):
                    @pl.when(step == 0)
                    def _():
                        a[...] = block

                    @pl.when(step > 0)
                    def _():
                        a[...] += block

                accesses.append(add)
        kernel(*accesses)

    results = pl.pallas_call(
        run,
        grid=(2 * half,),
        in_specs=[spec for a in arrays for spec in specs(a)],
        out_specs=[spec for o in outs for spec in specs(o)],
        out_shape=flat(outs),
        compiler_params=pltpu.CompilerParams(vmem_limit_bytes=32 * 2**20),
        cost_estimate=pl.CostEstimate(
            flops=20 * rows * width, bytes_accessed=12 * rows * width, transcendentals=rows
        ),
        name=name,
    )(*flat(arrays))
    results = list(results)
    return [
        (results.pop(0), results.pop(0)) if isinstance(o, tuple) else results.pop(0) for o in outs
    ]


def feed_kernel(count, *refs):
    seconds, grads = refs[:count], refs[count : 2 * count]
    up_ref, down_ref, bias_ref, before_ref = refs[2 * count : 2 * count + 4]
    mlps, backs = refs[2 * count + 4 : 3 * count + 4], refs[3 * count + 4 : 4 * count + 4]
    active_ref, upper_ref, sums_ref, second_ref, grad_ref, mlp_ref, back_ref = refs[4 * count + 4 :]
    step = pl.program_id(0)
    for k in range(count):

        @pl.when(step == k)
        def _(k=k):
            second_ref[...] = seconds[k][...]
            grad_ref[...] = grads[k][...]

    contract = (((1,), (1,)), ((), ()))
    upper = jnp.dot(second_ref[...], up_ref[...], preferred_element_type=F32) + bias_ref[...]
    active, slope = gelu_both(upper)
    active = active.astype(BF16)
    active_ref[...] = active
    grad_active = jnp.dot(grad_ref[...], down_ref[...], preferred_element_type=F32)
    grad_upper = (grad_active * slope).astype(BF16)
    upper_ref[...] = grad_upper
    back_ref[...] = lax.dot_general(
        grad_upper, up_ref[...], contract, preferred_element_type=F32
    ).astype(BF16)
    mlp_ref[...] = lax.dot_general(
        active, down_ref[...], contract, preferred_element_type=F32
    ).astype(BF16)
    for k in range(count):

        @pl.when(step == k)
        def _(k=k):
            mlps[k][...] = mlp_ref[...]
            backs[k][...] = back_ref[...]

    @pl.when(step == 0)
    def _():
        sums_ref[...] = before_ref[...]

    sums_ref[...] += jnp.sum(grad_upper.astype(F32), axis=0, keepdims=True)


def feed(tile, seconds, grads, weights, bias, before, name):
    count = len(seconds)
    width = seconds[0][0].shape[1]
    hidden = bias.shape[1]
    block = pl.BlockSpec((tile, width), lambda i: (0, 0))

    def at(k):
        return pl.BlockSpec((tile, width), lambda i: (k, 0))

    by_hidden = pl.BlockSpec((tile, hidden), lambda i: (i, 0))
    row = pl.BlockSpec((1, hidden), lambda i: (0, 0))
    results = pl.pallas_call(
        functools.partial(feed_kernel, count),
        grid=(count,),
        in_specs=[at(k) for _, k in seconds + grads]
        + [
            pl.BlockSpec((width, hidden), lambda i: (0, 0)),
            pl.BlockSpec((width, hidden), lambda i: (0, 1)),
            row,
            row,
        ],
        out_specs=[block] * (2 * count) + [by_hidden, by_hidden, row],
        out_shape=[jax.ShapeDtypeStruct((tile, width), BF16)] * (2 * count)
        + [
            jax.ShapeDtypeStruct((count * tile, hidden), BF16),
            jax.ShapeDtypeStruct((count * tile, hidden), BF16),
            jax.ShapeDtypeStruct((1, hidden), F32),
        ],
        scratch_shapes=[pltpu.VMEM((tile, width), BF16)] * 4,
        compiler_params=pltpu.CompilerParams(vmem_limit_bytes=50 * 2**20),
        cost_estimate=pl.CostEstimate(
            flops=8 * count * tile * width * hidden,
            bytes_accessed=16 * 2**20,
            transcendentals=count * tile * hidden,
        ),
        name=name,
    )(*(a for a, _ in seconds + grads), weights, weights, bias, before)
    return results[:count], results[count : 2 * count], results[-3], results[-2], results[-1]


def weight_kernel(blocks, groups, *refs):
    out_ref = refs[-1]
    rights = refs[2 * blocks : -1]
    hidden = rights[0].shape[1]
    for side in range(2):
        lefts = refs[side * blocks : (side + 1) * blocks]
        total = None
        at = 0
        for g, count in enumerate(groups):
            left = jnp.concatenate([lefts[at + k][...] for k in range(count)], axis=0)
            at += count
            term = lax.dot_general(
                left,
                rights[side * len(groups) + g][...],
                (((0,), (0,)), ((), ())),
                preferred_element_type=F32,
            )
            total = term if total is None else total + term
        out_ref[:, side * hidden : (side + 1) * hidden] = total.astype(BF16)


def weight_grads(rows, seconds, grads, uppers, actives):
    groups = [len(g) for g in seconds]
    lefts = [b for g in seconds for b in g] + [b for g in grads for b in g]
    blocks = sum(groups)
    width = lefts[0][0].shape[1]
    hidden = uppers[0].shape[1]
    tile = min(256, width)

    def at(k):
        return pl.BlockSpec((rows, tile), lambda i: (k, i))

    return pl.pallas_call(
        functools.partial(weight_kernel, blocks, groups),
        grid=(width // tile,),
        in_specs=[at(k) for _, k in lefts]
        + [pl.BlockSpec(r.shape, lambda i: (0, 0)) for r in uppers + actives],
        out_specs=pl.BlockSpec((tile, 2 * hidden), lambda i: (i, 0)),
        out_shape=jax.ShapeDtypeStruct((width, 2 * hidden), BF16),
        compiler_params=pltpu.CompilerParams(vmem_limit_bytes=50 * 2**20),
        cost_estimate=pl.CostEstimate(
            flops=4 * blocks * rows * width * hidden, bytes_accessed=20 * 2**20, transcendentals=0
        ),
        name="weight_grads",
    )(*(a for a, _ in lefts), *uppers, *actives)


def fill_bias(bias, masked, slope):
    size = bias.shape[0]
    key = lax.broadcasted_iota(jnp.int32, (size, size), 0)
    query = lax.broadcasted_iota(jnp.int32, (size, size), 1)
    value = key.astype(F32) * slope
    bias[...] = value
    masked[...] = jnp.where(key <= query, value, NEG)


def head_rows(block, head):
    half = block.shape[0] // 2
    rows = lax.broadcasted_iota(jnp.int32, block.shape, 0)
    keep = (rows < half) if head == 0 else (rows >= half)
    return jnp.where(keep, block, jnp.zeros_like(block))


def forward_kernel(
    place, slope_ref, q_ref, k_ref, v_ref, mixed_ref, full_ref, log_ref, bias, masked, values_t, *, scale, pair
):
    query_block = pl.program_id(0)
    me = place[0]
    size = bias.shape[1]
    half = q_ref.shape[0] // 2

    @pl.when(query_block == 0)
    def _():
        values_t[...] = v_ref[...].T
        for head in range(2):
            fill_bias(bias.at[head], masked.at[head], slope_ref[2 * pair + head])

    outputs = []
    logs = []
    for head in range(2):
        step = slope_ref[2 * pair + head] * size
        queries = head_rows(q_ref[...], head)

        def block(key_block, carry, bias_block, head=head, step=step, queries=queries):
            top, total, acc = carry
            at = pl.multiple_of((key_block ^ me) * size, size)
            raw = jnp.dot(k_ref[pl.ds(at, size), :], queries, preferred_element_type=F32)
            scores = raw * scale + bias_block
            base = key_block.astype(F32) * step
            new_top = jnp.maximum(top, jnp.max(scores, axis=0, keepdims=True) + base)
            weights = jnp.exp2(scores - (new_top - base))
            fade = jnp.exp2(top - new_top)
            total = total * fade + jnp.sum(weights, axis=0, keepdims=True)
            rows = values_t[head * half : (head + 1) * half, pl.ds(at, size)]
            acc = acc * fade + jnp.dot(rows, weights.astype(BF16), preferred_element_type=F32)
            return new_top, total, acc

        start = (
            jnp.full((1, size), NEG, F32),
            jnp.zeros((1, size), F32),
            jnp.zeros((half, size), F32),
        )
        carry = lax.fori_loop(
            0, query_block, lambda i, c, head=head, block=block: block(i, c, bias[head]), start
        )
        top, total, acc = block(query_block, carry, masked[head])
        outputs.append(acc / total)
        logs.append(top + jnp.log2(total))
    result = jnp.concatenate(outputs, axis=0)
    full_ref[...] = result
    mixed_ref[...] = result.astype(BF16)
    log_ref[...] = jnp.concatenate(logs, axis=0)


def backward_kernel(
    place,
    slope_ref,
    q_ref,
    k_ref,
    v_ref,
    g_ref,
    full_ref,
    log_ref,
    gq_ref,
    gk_ref,
    gv_ref,
    sums_ref,
    bias,
    masked,
    gq_acc,
    delta,
    *,
    scale,
    factor,
    pair,
):
    key_block = pl.program_id(0)
    blocks = pl.num_programs(0)
    me = place[0]
    size = bias.shape[1]
    half = q_ref.shape[0] // 2

    @pl.when(key_block == 0)
    def _():
        gq_acc[...] = jnp.zeros_like(gq_acc)
        for head in range(2):
            fill_bias(bias.at[head], masked.at[head], slope_ref[2 * pair + head])
            rows = slice(head * half, (head + 1) * half)
            delta[head : head + 1, :] = jnp.sum(
                g_ref[rows, :].astype(F32) * full_ref[rows, :], axis=0, keepdims=True
            )

    keys = k_ref[...]
    keys_t = keys.T
    values = v_ref[...]
    grad_k = jnp.zeros(keys.shape, F32)
    grad_v = jnp.zeros(keys.shape, F32)
    for head in range(2):
        base = key_block.astype(F32) * (slope_ref[2 * pair + head] * size)
        rows = slice(head * half, (head + 1) * half)

        def block(query_block, carry, bias_block, head=head, base=base, rows=rows):
            grad_k, grad_v = carry
            at = pl.multiple_of((query_block ^ me) * size, size)
            queries = head_rows(q_ref[:, pl.ds(at, size)], head)
            grads = head_rows(g_ref[:, pl.ds(at, size)], head)
            raw = jnp.dot(keys, queries, preferred_element_type=F32)
            log = log_ref[head : head + 1, pl.ds(at, size)] - base
            weights = jnp.exp2(raw * scale + (bias_block - log))
            along = jnp.dot(values, grads, preferred_element_type=F32)
            change = (weights * (along - delta[head : head + 1, pl.ds(at, size)])).astype(BF16)
            contract = (((1,), (1,)), ((), ()))
            grad_v = grad_v + lax.dot_general(
                weights.astype(BF16), grads, contract, preferred_element_type=F32
            )
            grad_k = grad_k + lax.dot_general(change, queries, contract, preferred_element_type=F32)
            gq_acc[rows, pl.ds(at, size)] += jnp.dot(
                keys_t[rows, :], change, preferred_element_type=F32
            )
            return grad_k, grad_v

        carry = block(key_block, (grad_k, grad_v), masked[head])
        grad_k, grad_v = lax.fori_loop(
            key_block + 1, blocks, lambda i, c, head=head, block=block: block(i, c, bias[head]), carry
        )
    low_k = (grad_k * factor).astype(BF16)
    low_v = grad_v.astype(BF16)
    gk_ref[...] = low_k
    gv_ref[...] = low_v
    sums = jnp.concatenate(
        [jnp.sum(low.astype(F32), axis=0, keepdims=True) for low in (low_k, low_v)], axis=0
    )

    @pl.when(key_block == 0)
    def _():
        sums_ref[...] = sums

    @pl.when(key_block > 0)
    def _():
        sums_ref[...] += sums

    @pl.when(key_block == blocks - 1)
    def _():
        gq_ref[...] = (gq_acc[...] * factor).astype(BF16)


def attend_forward(place, slopes, queries_t, keys, values, size, head_dim, pair):
    length = queries_t.shape[1]
    wide = 2 * head_dim
    along_q = pl.BlockSpec((wide, size), lambda i, me, s: (pair, i ^ me[0]))
    out_q = pl.BlockSpec((wide, size), lambda i, me, s: (0, i ^ me[0]))
    whole = pl.BlockSpec((length, wide), lambda i, me, s: (0, pair))
    return pl.pallas_call(
        functools.partial(forward_kernel, scale=LOG2E / math.sqrt(head_dim), pair=pair),
        grid_spec=pltpu.PrefetchScalarGridSpec(
            num_scalar_prefetch=2,
            grid=(length // size,),
            in_specs=[along_q, whole, whole],
            out_specs=[out_q, out_q, pl.BlockSpec((2, size), lambda i, me, s: (0, i ^ me[0]))],
            scratch_shapes=[
                pltpu.VMEM((2, size, size), F32),
                pltpu.VMEM((2, size, size), F32),
                pltpu.VMEM((wide, length), BF16),
            ],
        ),
        out_shape=[
            jax.ShapeDtypeStruct((wide, length), BF16),
            jax.ShapeDtypeStruct((wide, length), F32),
            jax.ShapeDtypeStruct((2, length), F32),
        ],
        compiler_params=pltpu.CompilerParams(vmem_limit_bytes=48 * 2**20),
        cost_estimate=pl.CostEstimate(
            flops=10 * 10**9, bytes_accessed=4 * 2**20, transcendentals=5 * 10**6
        ),
        name=f"attend_forward_{pair}",
    )(place, slopes, queries_t, keys, values)


def attend_backward(place, slopes, queries_t, keys, values, grads_t, full, logs, size, head_dim, pair):
    length = queries_t.shape[1]
    wide = 2 * head_dim
    along_k = pl.BlockSpec((size, wide), lambda i, me, s: (i ^ me[0], pair))
    out_k = pl.BlockSpec((size, wide), lambda i, me, s: (i ^ me[0], 0))
    all_q = pl.BlockSpec((wide, length), lambda i, me, s: (pair, 0))
    whole = pl.BlockSpec((wide, length), lambda i, me, s: (0, 0))
    return pl.pallas_call(
        functools.partial(
            backward_kernel,
            scale=LOG2E / math.sqrt(head_dim),
            factor=1.0 / math.sqrt(head_dim),
            pair=pair,
        ),
        grid_spec=pltpu.PrefetchScalarGridSpec(
            num_scalar_prefetch=2,
            grid=(length // size,),
            in_specs=[
                all_q,
                along_k,
                along_k,
                whole,
                whole,
                pl.BlockSpec((2, length), lambda i, me, s: (0, 0)),
            ],
            out_specs=[whole, out_k, out_k, pl.BlockSpec((2, wide), lambda i, me, s: (0, 0))],
            scratch_shapes=[
                pltpu.VMEM((2, size, size), F32),
                pltpu.VMEM((2, size, size), F32),
                pltpu.VMEM((wide, length), F32),
                pltpu.VMEM((2, length), F32),
            ],
        ),
        out_shape=[
            jax.ShapeDtypeStruct((wide, length), BF16),
            jax.ShapeDtypeStruct((length, wide), BF16),
            jax.ShapeDtypeStruct((length, wide), BF16),
            jax.ShapeDtypeStruct((2, wide), F32),
        ],
        compiler_params=pltpu.CompilerParams(vmem_limit_bytes=48 * 2**20),
        cost_estimate=pl.CostEstimate(
            flops=20 * 10**9, bytes_accessed=6 * 2**20, transcendentals=5 * 10**6
        ),
        name=f"attend_backward_{pair}",
    )(place, slopes, queries_t, keys, values, grads_t, full, logs)


def swap(value, axis, distance):
    size = lax.axis_size(axis)
    return lax.ppermute(value, axis, [(i, i ^ distance) for i in range(size)])


def after(value, *earlier):
    return lax.optimization_barrier((value,) + earlier)[0]


def exchange_blocks(parts):
    return [parts[0]] + [swap(parts[j], "tensor", j) for j in range(1, 4)]


def chip_sum(far, far_near):
    return (far.astype(F32) + swap(far_near, "tensor", 1).astype(F32)).astype(BF16)


def sum_over(value, axes):
    for axis in axes:
        size = lax.axis_size(axis)
        distance = 1
        while distance < size:
            if distance * 4 <= size:
                one, two, three = (swap(value, axis, distance * k) for k in (1, 2, 3))
                value = (value + one) + (two + three)
                distance *= 4
            else:
                value = value + swap(value, axis, distance)
                distance *= 2
    return value


def gather_dp(shard):
    count = lax.axis_size("dp")
    me = lax.axis_index("dp")
    rows = shard.shape[0]
    blocks = [(0, shard)]
    distance = count // 2
    while distance > 1:
        blocks = blocks + [(o + distance, swap(block, "dp", distance)) for o, block in blocks]
        distance //= 2
    whole = jnp.zeros((count * rows, shard.shape[1]), shard.dtype)
    for offset, block in blocks:
        for o, piece in ((offset, block), (offset + 1, swap(block, "dp", 1))):
            whole = lax.dynamic_update_slice(whole, piece, ((me ^ o) * rows, 0))
    return whole, [block for _, block in blocks[1:]]


def scatter_dp_parts(whole):
    count = lax.axis_size("dp")
    me = lax.axis_index("dp")
    rows, width = whole.shape[0] // count, whole.shape[1]

    def blocks(start):
        return jnp.concatenate(
            [
                lax.dynamic_slice(whole, ((me ^ d) * rows, 0), (rows, width))
                for d in range(start, count, 2)
            ],
            axis=0,
        )

    return blocks(0), blocks(1)


def scatter_dp_last(even):
    parts = rows_of(even, lax.axis_size("dp") // 2)
    total = parts[0].astype(F32)
    for k, part in enumerate(parts[1:]):
        total = total + swap(part, "dp", 2 * k + 2).astype(F32)
    return total


def rows_of(value, count):
    size = value.shape[0] // count
    return [value[i * size : (i + 1) * size] for i in range(count)]


def dot(a, b, ca, cb):
    return lax.dot_general(a, b, (((ca,), (cb,)), ((), ())), preferred_element_type=F32)


def body(
    hidden_in,
    norm_gain,
    norm_shift,
    qkv_weight,
    qv_bias,
    out_weight,
    out_bias,
    up_weight,
    up_bias,
    down_weight,
    cotangent,
):
    rows, width = hidden_in.shape
    tensor_size = lax.axis_size("tensor")
    heads_wide = qkv_weight.shape[2]
    hidden_units = up_weight.shape[1]
    local_heads = HEADS // tensor_size
    head_dim = heads_wide // local_heads
    pairs = local_heads // 2
    wide = 2 * head_dim
    me = lax.axis_index("tensor").astype(jnp.int32)
    place = me.reshape(1)
    head_ids = me * local_heads + jnp.arange(local_heads, dtype=jnp.int32)
    slopes = jnp.exp2(-8.0 * (head_ids.astype(F32) + 1.0) / HEADS) * LOG2E
    part = rows // 2
    stat = functools.partial(row_call, rows=rows, width=width)
    row_f32 = jax.ShapeDtypeStruct((rows, width), F32)
    row_bf16 = jax.ShapeDtypeStruct((rows, width), BF16)
    part_bf16 = jax.ShapeDtypeStruct((part, width), BF16)
    four_f32 = jax.ShapeDtypeStruct((4, width), F32)

    first_shard = jnp.concatenate(
        [qkv_weight[0], qkv_weight[1], qkv_weight[2], out_weight.T], axis=1
    )
    second_shard = jnp.concatenate([up_weight, down_weight.T], axis=1)
    first_full, first_others = gather_dp(first_shard)
    second_full = lax.all_gather(after(second_shard, *first_others), "dp", axis=0, tiled=True)

    (normed,) = stat(
        first_norm_kernel, arrays=[hidden_in, norm_gain, norm_shift], outs=[row_bf16], name="norm_one"
    )
    normed_far = after(swap(normed, "tensor", 2), *first_others)
    normed_near = swap(normed, "tensor", 1)
    normed_rows = jnp.concatenate(
        [normed, normed_near, normed_far, swap(normed_far, "tensor", 1)], axis=0
    )
    grads_far = swap(cotangent, "tensor", 2)
    normed_rows = after(normed_rows, grads_far)
    grads_near = swap(cotangent, "tensor", 1)
    grads_far_near = swap(grads_far, "tensor", 1)

    w_query, w_key, w_value = (
        first_full[:, c * heads_wide : (c + 1) * heads_wide] for c in range(3)
    )
    queries_t = (dot(w_query, normed_rows, 0, 1) + qv_bias[0][:, None]).astype(BF16)
    keys = dot(normed_rows, w_key, 1, 0).astype(BF16)
    values = (dot(normed_rows, w_value, 1, 0) + qv_bias[1]).astype(BF16)
    out_mine = first_full[:, 3 * heads_wide :]
    out_far = swap(out_mine, "tensor", 2)
    kept = []
    mixed_parts = [[] for _ in range(tensor_size)]
    received = out_far
    for pair in range(pairs):
        mixed_t, mixed_full, logs = attend_forward(
            place,
            slopes,
            queries_t if pair == 0 else after(queries_t, out_far, mixed_full),
            keys,
            values,
            rows,
            head_dim,
            pair,
        )
        if pair > 0:
            mixed_t = after(mixed_t, *received)
        kept.append((mixed_full, logs))
        parts = [mixed_t[:, j * rows : (j + 1) * rows] for j in range(tensor_size)]
        received = exchange_blocks(parts)
        for j, block in enumerate(received):
            mixed_parts[j].append(block)
    out_full = jnp.concatenate(
        [out_mine, swap(out_mine, "tensor", 1), out_far, swap(out_far, "tensor", 1)], axis=1
    )
    mixed_all = jnp.concatenate([block for group in mixed_parts for block in group], axis=0)
    attn_sum = dot(mixed_all, out_full, 0, 1)
    middle, second = stat(
        second_norm_kernel,
        arrays=[hidden_in, attn_sum, out_bias, norm_gain, norm_shift],
        outs=[row_f32, (part_bf16, part_bf16)],
        name="norm_two",
    )

    up_bias_row = up_bias.reshape(1, hidden_units)
    far_chunks = [swap(second[c], "tensor", 2) for c in range(2)]
    seconds = [[(block, 0) for block in second]]
    seconds[0] += [(swap(block, "tensor", 1), 0) for block in second]
    grads = [[(g, c) for g in (cotangent, grads_near) for c in range(2)]]
    mlp_a, back_a, active, upper, sums_up = feed(
        part, seconds[0], grads[0], second_full, up_bias_row, jnp.zeros_like(up_bias_row), "feed_near"
    )
    actives, uppers = [active], [upper]
    mlps, back_fars = [], []
    earlier = (mlp_a[0],)
    for c in range(2):
        far = after(far_chunks[c], *earlier)
        pair_c = [(far, 0), (swap(far, "tensor", 1), 0)]
        if c > 0:
            pair_c[0] = (after(far, mine), 0)
        grads_c = [(grads_far, c), (grads_far_near, c)]
        mlp_c, back_c, active, upper, sums_up = feed(
            part, pair_c, grads_c, second_full, up_bias_row, sums_up, f"feed_far_{c}"
        )
        earlier = (mlp_c[0],)
        seconds.append(pair_c)
        grads.append(grads_c)
        actives.append(active)
        uppers.append(upper)
        mlps.append(mlp_c)
        mine = chip_sum(back_c[0], after(back_c[1], *back_fars))
        back_fars.append(swap(mine, "tensor", 2))
    back_near = tuple(swap(back_a[2 + c], "tensor", 1) for c in range(2))

    uppers[0] = after(uppers[0], back_fars[0], mine)
    grad_second_w = weight_grads(part, seconds, grads, uppers, actives)
    grad_second_w = lax.psum_scatter(
        grad_second_w, "dp", scatter_dimension=0, tiled=True
    ).astype(F32)
    grad_up_weight = grad_second_w[:, :hidden_units]
    grad_down_weight = grad_second_w[:, hidden_units:].T

    grad_middle, grad_attn, early = stat(
        second_back_kernel,
        arrays=[middle, cotangent, tuple(back_a[:2]), back_near, tuple(back_fars), norm_gain],
        outs=[row_f32, row_bf16, four_f32],
        name="norm_two_back",
    )
    mixed_grads = dot(out_full, grad_attn, 0, 1).astype(BF16)
    mlps = [lax.optimization_barrier((*m, grad_attn))[:2] for m in mlps]
    mlp_a = lax.optimization_barrier((*mlp_a, grad_attn))[:4]
    grads_t = []
    for pair in range(pairs):
        parts = [
            mixed_grads[j * heads_wide + pair * wide : j * heads_wide + (pair + 1) * wide]
            for j in range(tensor_size)
        ]
        grads_t.append(jnp.concatenate(exchange_blocks(parts), axis=1))

    out_partial = dot(after(grad_attn, mixed_grads), mixed_all, 0, 1).astype(BF16)
    out_cols = [out_partial[:, j * heads_wide : (j + 1) * heads_wide] for j in range(tensor_size)]
    out_mine_sum = chip_sum(out_cols[2], out_cols[3])
    out_far_sum = swap(out_mine_sum, "tensor", 2)
    mlp_mine_sum = jnp.concatenate([chip_sum(m[0], m[1]) for m in mlps], axis=0)
    mlp_far = swap(after(mlp_mine_sum, out_far_sum), "tensor", 2)
    mlp_near = swap(jnp.concatenate(mlp_a[2:], axis=0), "tensor", 1)
    mlp_own = jnp.concatenate(mlp_a[:2], axis=0)
    block_out = (
        middle
        + (mlp_own.astype(F32) + mlp_near.astype(F32) + mlp_far.astype(F32))
        + out_bias[1]
    )
    low = []
    first_sums = []
    for pair in range(pairs):
        grads_pair = grads_t[pair]
        if pair == 0:
            grads_pair = after(grads_pair, out_mine_sum, mlp_mine_sum)
        else:
            grads_pair = after(grads_pair, low[-1][0], out_far_sum)
        mixed_full, logs = kept[pair]
        low.append(
            attend_backward(
                place, slopes, queries_t, keys, values, grads_pair, mixed_full, logs, rows, head_dim, pair
            )
        )
    sent = []
    piece_groups = []
    for pair in range(pairs):
        if pair == pairs - 1 and pair > 0:
            held = lax.optimization_barrier((*low[pair], mlp_far, *(x[1] for x in sent)))
            low[pair] = held[:4]
            sent = [(x[0], arrived) for x, arrived in zip(sent, held[5:])]
        query_p, key_p, value_p, _ = low[pair]
        pieces = [
            dot(normed_rows, query_p, 0, 1).astype(BF16),
            dot(normed_rows, key_p, 0, 0).astype(BF16),
            dot(normed_rows, value_p, 0, 0).astype(BF16),
        ]
        piece_groups.append(list(pieces))
        if pair == pairs - 1:
            pieces.append(
                (
                    out_cols[0].astype(F32)
                    + swap(out_cols[1], "tensor", 1).astype(F32)
                    + out_far_sum.astype(F32)
                ).astype(BF16)
            )
        keep, send = scatter_dp_parts(jnp.concatenate(pieces, axis=1))
        sent.append((keep, swap(send, "dp", 1)))

    query_low = after(jnp.concatenate([g[0] for g in low], axis=0), send)
    key_low = jnp.concatenate([g[1] for g in low], axis=1)
    value_low = jnp.concatenate([g[2] for g in low], axis=1)

    def normed_grads(at, query_low):
        return (
            dot(query_low[:, at], w_query, 0, 1)
            + dot(key_low[at], w_key, 1, 1)
            + dot(value_low[at], w_value, 1, 1)
        ).astype(BF16)

    half = 2 * rows
    far_grads = normed_grads(slice(half, 2 * half), query_low)
    first_mine = chip_sum(far_grads[:rows], far_grads[rows:])
    first_far = swap(first_mine, "tensor", 2)
    near_grads = normed_grads(slice(0, half), after(query_low, first_mine))
    first_near = swap(near_grads[rows:], "tensor", 1)

    for keep, arrived in sent:
        arrived = after(arrived, first_mine)
        first_sums.append((keep.astype(F32) + arrived.astype(F32)).astype(BF16))

    query_sums, value_sums = [], []
    gain_sum, shift_sum = 0.0, 0.0
    for pair in range(pairs):
        sums_p = after(low[pair][3], first_mine)
        query_sums.append(jnp.sum(after(low[pair][0], first_mine).astype(F32), axis=1))
        value_sums.append(sums_p[1])
        column_sums = (query_sums[-1], sums_p[0], sums_p[1])
        for weight, piece, column in zip(
            (w_query, w_key, w_value), piece_groups[pair], column_sums
        ):
            weight_p = weight[:, pair * wide : (pair + 1) * wide].astype(F32)
            gain_sum = gain_sum + jnp.sum(weight_p * after(piece, first_mine).astype(F32), axis=1)
            shift_sum = shift_sum + jnp.sum(weight_p * column[None, :], axis=1)
    gain_sum = (gain_sum - norm_shift[0] * shift_sum) / norm_gain[0]

    first_sums = scatter_dp_last(jnp.concatenate(first_sums, axis=1))
    grad_qkv = jnp.stack(
        [
            jnp.concatenate(
                [
                    first_sums[:, (3 * pair + c) * wide : (3 * pair + c + 1) * wide]
                    for pair in range(pairs)
                ],
                axis=1,
            )
            for c in range(3)
        ]
    )
    grad_out_weight = first_sums[:, 3 * heads_wide :].T

    (grad_in,) = stat(
        first_back_kernel,
        arrays=[hidden_in, grad_middle, near_grads[:rows], first_near, first_far, norm_gain],
        outs=[row_f32],
        name="norm_one_back",
    )
    lanes = 128
    whole_sums = jnp.concatenate([early, gain_sum[None], shift_sum[None]], axis=0).reshape(-1, lanes)
    split_sums = jnp.concatenate(query_sums + value_sums + [sums_up[0]]).reshape(-1, lanes)
    sums = sum_over(jnp.concatenate([whole_sums, split_sums], axis=0), ("dp",))
    whole_sums = sum_over(sums[: whole_sums.shape[0]], ("tensor",)).reshape(-1, width)
    split_sums = sums[whole_sums.size // lanes :].reshape(-1)
    return (
        block_out,
        grad_in,
        jnp.stack([whole_sums[4], whole_sums[0]]),
        jnp.stack([whole_sums[5], whole_sums[1]]),
        grad_qkv,
        split_sums[: 2 * heads_wide].reshape(2, heads_wide),
        grad_out_weight,
        whole_sums[2:4],
        grad_up_weight,
        split_sums[2 * heads_wide :],
        grad_down_weight,
    )


def solution(mesh):
    return jax.shard_map(
        body,
        mesh=mesh,
        in_specs=(
            P(("dp", "tensor"), None),
            P(),
            P(),
            P(None, "dp", "tensor"),
            P(None, "tensor"),
            P("tensor", "dp"),
            P(),
            P("dp", "tensor"),
            P("tensor"),
            P("tensor", "dp"),
            P(("dp", "tensor"), None),
        ),
        out_specs=(
            P(("dp", "tensor"), None),
            P(("dp", "tensor"), None),
            P(),
            P(),
            P(None, "dp", "tensor"),
            P(None, "tensor"),
            P("tensor", "dp"),
            P(),
            P("dp", "tensor"),
            P("tensor"),
            P("tensor", "dp"),
        ),
        check_vma=False,
    )
```

time: 526 us -> 379 us (0.72)
  waiting for transfers between devices: 216 us -> 79.9 us
  Pallas kernels: 66.9 us -> 130 us
  matrix products: 84.1 us -> 22.2 us
  blocking collectives: 32.1 us -> 0 us
  starting transfers between devices: 31.1 us -> 53.1 us
  local copies, waits for them, and re-layouts: 33.6 us -> 44 us
  other arithmetic: 38.9 us -> 29.9 us
    dot_general x18, matrix products: 84.1 us -> 22.2 us  [dot(): lax.dot_general(a, b, (((ca,), (cb,)), ((), ())), preferred_element_type=...]
    ppermute x46 -> x62, waiting for transfers between devices: 142 us -> 79.8 us  [swap(): return lax.ppermute(value, axis, [(i, i ^ distance) for i in range(size)])]
    pallas_call x0 -> x8, Pallas kernels: none -> 61.4 us  [the longest x3 34.1 us: feed(): pl.pallas_call(functools.partial(feed_kernel, count), grid=(count,), in_s...]
    reduce_scatter x2 -> x1, waiting for transfers between devices: 53.9 us -> 0.01 us  [body(): lax.psum_scatter(grad_second_w, 'dp', scatter_dimension=0, tiled=True)]
    all_gather x1 -> x0, blocking collectives: 32.1 us -> none  [body(): out_mine = lax.all_gather(out_weight, 'dp', axis=1, tiled=True)]
    ppermute x46 -> x62, starting transfers between devices: 30 us -> 53 us  [swap(): return lax.ppermute(value, axis, [(i, i ^ distance) for i in range(size)])]
    unnamed x9 -> x2, waiting for transfers between devices: 20 us -> 0.03 us
    reduce_sum x8 -> x4, other arithmetic: 15.5 us -> 1.29 us  [the longest x2 0.98 us: body(): jnp.sum(weight_p * after(piece, first_mine).astype(F32), axis=1)]
  transfers between devices with their start and end apart: 53 -> 64, of which waited for: 20 -> 23; matrix products, arithmetic and copies ran while one was open for 29% -> 18% of each run, Pallas kernels for 13% -> 34%
where the time goes in v2:
time: 379 us; the launch traced here: 375 us
  Pallas kernels  130 us (34%)
  waiting for transfers between devices  79.9 us (21%)
  starting transfers between devices  53.1 us (14%)
  local copies, waits for them, and re-layouts  44 us (12%)
  other arithmetic  29.9 us (8%)
  matrix products  22.2 us (6%)
  between operations  15.9 us (4%)
    ppermute x62, waiting for transfers between devices, swap(): return lax.ppermute(value, axis, [(i, i ^ distance) for i in range(size)])  79.8 us
    ppermute x62, starting transfers between devices, swap(): return lax.ppermute(value, axis, [(i, i ^ distance) for i in range(size)])  53 us
    pallas_call x2, Pallas kernels, attend_backward(): pl.pallas_call(functools.partial(backward_kernel, scale=LOG2E / math.sqrt...  41 us
    pallas_call x3, Pallas kernels, feed(): pl.pallas_call(functools.partial(feed_kernel, count), grid=(count,), in_s...  34.1 us
    unnamed x208, local copies, waits for them, and re-layouts  29.4 us
    pallas_call x2, Pallas kernels, attend_forward(): pl.pallas_call(functools.partial(forward_kernel, scale=LOG2E / math.sqrt(...  28 us
    dot_general x18, matrix products, dot(): lax.dot_general(a, b, (((ca,), (cb,)), ((), ())), preferred_element_type=...  22.2 us
    pallas_call x1, Pallas kernels, weight_grads(): pl.pallas_call(functools.partial(weight_kernel, blocks, groups), grid=(wi...  14.8 us
  transfers between devices with their start and end apart: 64, of which 23 were waited for; matrix products, arithmetic and copies ran while one was open for 18% of the time, Pallas kernels for 34%

profile of v2, /device:TPU:0, one launch (start us, length us, event | category | flops | bytes accessed | tf_op | source)
XLA Modules:
  0.0 375.3 jit_solution(377067885448896084)
XLA Ops:
  11.0 3.0 collective-permute-start.8
  15.4 2.6 collective-permute-start.1
  18.0 1.6 collective-permute-start.3
  19.6 10.5 %collective-permute-done.1 = bf16[128,1024]{0,1:T(8,128)(2,1)} collective-permute-done((bf16[128,1024]{0,1:T(8,128)(2,1)}, bf16[128,1024]{0,1:T(8,128)(2,1)}, u32[]{:S(2)}, u32[]{:S(2)}) %collective-permute-start.1) | collective-permute-done | bytes 262176 | tf_op jit(solution)/shard_map/ppermute | solution.py:524
  31.8 1.8 pad_maximum_fusion.8
  33.5 4.0 %collective-permute-done.5 = bf16[128,1024]{0,1:T(8,128)(2,1)} collective-permute-done((bf16[128,1024]{0,1:T(8,128)(2,1)}, bf16[128,1024]{0,1:T(8,128)(2,1)}, u32[]{:S(2)}, u32[]{:S(2)}) %collective-permute-start.5) | collective-permute-done | bytes 262176 | tf_op jit(solution)/shard_map/ppermute | solution.py:524
  37.7 1.6 collective-permute-start
  40.3 6.7 %collective-permute-done = bf16[128,1024]{0,1:T(8,128)(2,1)S(1)} collective-permute-done((bf16[128,1024]{0,1:T(8,128)(2,1)}, bf16[128,1024]{0,1:T(8,128)(2,1)S(1)}, u32[]{:S(2)}, u32[]{:S(2)}) %collective-permute-start) | collective-permute-done | bytes 262176 | tf_op jit(solution)/shard_map/ppermute | solution.py:524
  47.0 1.5 collective-permute-start.4
  49.7 6.1 %collective-permute-done.2 = bf16[128,1024]{0,1:T(8,128)(2,1)} collective-permute-done((bf16[128,1024]{0,1:T(8,128)(2,1)}, bf16[128,1024]{0,1:T(8,128)(2,1)}, u32[]{:S(2)}, u32[]{:S(2)}) %collective-permute-start.2) | collective-permute-done | bytes 262176 | tf_op jit(solution)/shard_map/ppermute | solution.py:524
  55.8 2.5 collective-permute-start.6
  60.4 3.5 collective-permute-done.4
  65.0 4.0 %collective-permute-done.6 = bf16[128,1024]{0,1:T(8,128)(2,1)S(1)} collective-permute-done((bf16[128,1024]{0,1:T(8,128)(2,1)}, bf16[128,1024]{0,1:T(8,128)(2,1)S(1)}, u32[]{:S(2)}, u32[]{:S(2)}) %collective-permute-start.6) | collective-permute-done | bytes 262176 | tf_op jit(solution)/shard_map/ppermute | solution.py:524
  69.8 2.4 pad_maximum_fusion
  72.2 1.3 convolution_convert_fusion.k_ref
  73.6 1.3 fusion.q_ref
  74.9 1.3 fusion.1.v_ref
  76.2 14.0 %attend_forward_0.1 = (bf16[128,2048]{1,0:T(8,128)(2,1)S(1)}, f32[128,2048]{1,0:T(8,128)S(1)}, f32[2,2048]{1,0:T(2,128)S(1)}) custom-call(s32[1]{0:T(128)} %bitcast.place, f32[4]{0:T(128)S(1)} %exponential_multiply_fusion.slope_ref, bf16[256,2048]{1,0:T(8,128)(2,1)S(1)} %fusion.q_ref, bf16[2048,256]{1,0:T(8,128)(2,1)S(1)} %convolution_convert_fusion.k_ref, ...), custom_call_target="tpu_custom_call" | custom-call | flops 10000000000 | bytes 4194304 | tf_op jit(solution)/shard_map/attend_forward_0/pallas_call | solution.py:449
  90.4 1.5 collective-permute-start.13
  92.3 14.0 %attend_forward_1.1 = (bf16[128,2048]{1,0:T(8,128)(2,1)S(1)}, f32[128,2048]{1,0:T(8,128)S(1)}, f32[2,2048]{1,0:T(2,128)S(1)}) custom-call(s32[1]{0:T(128)} %bitcast.place, f32[4]{0:T(128)S(1)} %exponential_multiply_fusion.slope_ref, bf16[256,2048]{1,0:T(8,128)(2,1)S(1)} %fusion.q_ref, bf16[2048,256]{1,0:T(8,128)(2,1)S(1)} %convolution_convert_fusion.k_ref, ...), custom_call_target="tpu_custom_call" | custom-call | flops 10000000000 | bytes 4194304 | tf_op jit(solution)/shard_map/attend_forward_1/pallas_call | solution.py:449
  107.5 1.4 collective-permute-start.16
  109.5 4.4 %collective-permute-done.16 = bf16[128,512]{1,0:T(8,128)(2,1)S(1)} collective-permute-done((bf16[128,512]{1,0:T(8,128)(2,1)S(1)}, bf16[128,512]{1,0:T(8,128)(2,1)S(1)}, u32[]{:S(2)}, u32[]{:S(2)}) %collective-permute-start.16) | collective-permute-done | bytes 131104 | tf_op jit(solution)/shard_map/ppermute | solution.py:524
  113.9 1.9 collective-permute-done.17
  117.7 1.3 fusion.39.refs_1_
  119.1 2.3 norm_two.1
  124.2 16.1 %feed_near.1 = (bf16[256,1024]{1,0:T(8,128)(2,1)S(1)}, bf16[256,1024]{1,0:T(8,128)(2,1)S(1)}, bf16[256,1024]{1,0:T(8,128)(2,1)S(1)}, bf16[256,1024]{1,0:T(8,128)...) custom-call(bf16[256,1024]{1,0:T(8,128)(2,1)} %get-tuple-element.105, ...), custom_call_target="tpu_custom_call" | custom-call | flops 8589934592 | bytes 16777216 | tf_op jit(solution)/shard_map/feed_near/pallas_call | solution.py:208
  147.3 9.0 %feed_far_0.1 = (bf16[256,1024]{1,0:T(8,128)(2,1)S(1)}, bf16[256,1024]{1,0:T(8,128)(2,1)S(1)}, bf16[256,1024]{1,0:T(8,128)(2,1)S(1)}, bf16[256,1024]{1,0:T(8,128...) custom-call(bf16[256,1024]{1,0:T(8,128)(2,1)} %collective-permute-done.25.refs_0_.refs_4_, ...), custom_call_target="tpu_custom_call" | custom-call | flops 4294967296 | bytes 16777216 | tf_op jit(solution)/shard_map/feed_far_0/pallas_call | solution.py:208
  157.4 2.1 collective-permute-done.30.refs_0_.refs_6_
  161.4 9.1 %feed_far_1.1 = (bf16[256,1024]{1,0:T(8,128)(2,1)S(1)}, bf16[256,1024]{1,0:T(8,128)(2,1)S(1)}, bf16[256,1024]{1,0:T(8,128)(2,1)S(1)}, bf16[256,1024]{1,0:T(8,128...) custom-call(bf16[256,1024]{1,0:T(8,128)(2,1)S(1)} %collective-permute-done.30.refs_0_.refs_6, ...), custom_call_target="tpu_custom_call" | custom-call | flops 4294967296 | bytes 16777216 | tf_op jit(solution)/shard_map/feed_far_1/pallas_call | solution.py:208
  172.1 2.0 collective-permute-done.29.refs_6_
  175.5 2.1 collective-permute-done.32
  179.8 14.8 %weight_grads.1 = bf16[1024,2048]{1,0:T(8,128)(2,1)} custom-call(bf16[256,1024]{1,0:T(8,128)(2,1)} %get-tuple-element.105.refs_0_, bf16[256,1024]{1,0:T(8,128)(2,1)S(1)} %copy-done.36, bf16[256,1024]{1,0:T(8,128)(2,1)} %collective-permute-done.20.refs_2_, bf16[256,1024]{1,0:T(8,128)(2,1)} %collective-permute-done.21.refs_3_, ...), custom_call_target="tpu_custom_call" | custom-call | flops 8589934592 | bytes 20971520 | tf_op jit(solution)/shard_map/weight_grads/pallas_call | solution.py:269
  197.8 4.6 %norm_two_back.1 = (f32[512,1024]{1,0:T(8,128)S(1)}, bf16[512,1024]{1,0:T(8,128)(2,1)S(1)}, f32[4,1024]{1,0:T(4,128)S(1)}) custom-call(f32[512,1024]{1,0:T(8,128)S(1)} %get-tuple-element.104.refs_0_, bf16[512,1024]{1,0:T(8,128)(2,1)} %refs_9_.1, bf16[256,1024]{1,0:T(8,128)(2,1)S(1)} %copy-done.17, bf16[256,1024]{1,0:T(8,128)(2,1)S(1)} %copy-done.19, ...), custom_call_target="tpu_custom_call" | custom-call | flops 10485760 | bytes 6291456 | tf_op jit(solution)/shard_map/norm_two_back/pallas_call | solution.py:138
  202.4 1.3 convolution_convert_fusion.2
  210.5 2.3 collective-permute-done.45
  212.8 1.9 collective-permute-start.42
  214.7 1.5 collective-permute-done.44
  218.0 1.6 collective-permute-start.35
  219.5 2.2 collective-permute-done.41
  226.8 20.5 %attend_backward_0.1 = (bf16[128,2048]{1,0:T(8,128)(2,1)S(1)}, bf16[2048,128]{1,0:T(8,128)(2,1)S(1)}, bf16[2048,128]{1,0:T(8,128)(2,1)S(1)}, f32[2,128]{1,0:T(2,128)S(1)}) custom-call(s32[1]{0:T(128)} %bitcast.place, f32[4]{0:T(128)S(1)} %exponential_multiply_fusion.slope_ref, bf16[256,2048]{1,0:T(8,128)(2,1)S(1)} %copy-done.42, ...), custom_call_target="tpu_custom_call" | custom-call | flops 20000000000 | bytes 6291456 | tf_op jit(solution)/shard_map/attend_backward_0/pallas_call | solution.py:482
  251.5 1.5 collective-permute-start.46
  255.0 20.4 %attend_backward_1.1 = (bf16[128,2048]{1,0:T(8,128)(2,1)S(1)}, bf16[2048,128]{1,0:T(8,128)(2,1)S(1)}, bf16[2048,128]{1,0:T(8,128)(2,1)S(1)}, f32[2,128]{1,0:T(2,128)S(1)}) custom-call(s32[1]{0:T(128)} %bitcast.place, f32[4]{0:T(128)S(1)} %exponential_multiply_fusion.slope_ref, bf16[256,2048]{1,0:T(8,128)(2,1)S(1)} %copy-done.42, ...), custom_call_target="tpu_custom_call" | custom-call | flops 20000000000 | bytes 6291456 | tf_op jit(solution)/shard_map/attend_backward_1/pallas_call | solution.py:482
  275.4 1.7 add_convert_fusion.4
  277.1 1.6 collective-permute-done.39
  287.0 1.3 copy-done.53
  290.0 4.0 %fusion.18 = f32[1024,1024]{1,0:T(8,128)} fusion(bf16[2048,256]{1,0:T(8,128)(2,1)} %copy-done.58, bf16[1024,1024]{0,1:T(8,128)(2,1)} %copy-done.50), kind=kOutput, calls=%fused_computation.68 | convolution fusion | flops 536870912 | bytes 5242880 | tf_op jit(solution)/shard_map/dot_general | solution.py:601
  294.0 3.6 add_add_fusion
  297.7 2.7 add_convert_fusion.2
  303.0 1.7 collective-permute-start.52
  304.7 1.3 collective-permute-start.53
  306.5 1.9 fusion.26
  308.9 1.8 add_convert_fusion
  311.9 1.3 add_convert_fusion.3
  313.3 1.3 add_convert_fusion.10
  314.7 3.4 collective-permute-start.54
  323.5 3.2 collective-permute-done.56
  326.7 4.3 %collective-permute-start.61 = (bf16[128,1024]{0,1:T(8,128)(2,1)}, bf16[128,1024]{0,1:T(8,128)(2,1)}, u32[]{:S(2)}, u32[]{:S(2)}) collective-permute-start(bf16[128,1024]{0,1:T(8,128)(2,1)} %get-tuple-element.219), channel_id=1, source_target_pairs={{0,24},{4,28},{8,16},{12,20},{16,8},{20,12},{24,0},{28,4},{1,25},{... | collective-permute-start | bytes 786440 | tf_op jit(solution)/shard_map/ppermute | solution.py:524
  334.2 4.5 %collective-permute-done.61 = bf16[128,1024]{0,1:T(8,128)(2,1)} collective-permute-done((bf16[128,1024]{0,1:T(8,128)(2,1)}, bf16[128,1024]{0,1:T(8,128)(2,1)}, u32[]{:S(2)}, u32[]{:S(2)}) %collective-permute-start.61) | collective-permute-done | bytes 262176 | tf_op jit(solution)/shard_map/ppermute | solution.py:524
  338.7 14.0 %collective-permute-done.60 = bf16[128,1024]{0,1:T(8,128)(2,1)} collective-permute-done((bf16[128,1024]{0,1:T(8,128)(2,1)}, bf16[128,1024]{0,1:T(8,128)(2,1)}, u32[]{:S(2)}, u32[]{:S(2)}) %collective-permute-start.60) | collective-permute-done | bytes 262176 | tf_op jit(solution)/shard_map/ppermute | solution.py:524
  352.6 1.3 convert_add_fusion
  355.6 1.9 copy.27
  357.5 1.6 slice_bitcast_fusion.1
  359.1 1.6 copy-done.7
  360.7 4.5 %norm_one_back.1 = f32[512,1024]{1,0:T(8,128)} custom-call(bf16[512,1024]{1,0:T(8,128)(2,1)S(1)} %copy-done.1, f32[512,1024]{1,0:T(8,128)S(1)} %copy-done.7, bf16[512,1024]{1,0:T(8,128)(2,1)S(1)} %get-tuple-element.207.refs_2_, bf16[512,1024]{1,0:T(8,128)(2,1)} %collective-permute-done.49.refs_3_, bf16[512,1024]{1,0:T(8,128)(2,1)S(1)} %collective-permute-done.50.refs_4_, ...), custom_call_target="tpu_custom_call" | custom-call | flops 10485760 | bytes 6291456 | tf_op jit(solution)/shard_map/norm_one_back/pallas_call | solution.py:138
  (388 shorter events, 85.6 us)
Async XLA Ops:
  7.2 117.0 %all-gather.2.cloned.1.call-start = ((), (), s32[]{:S(2)}) async-start(), calls=%async_computation.1 | async-start | bytes 4718592 | tf_op jit(solution)/shard_map/all_gather | solution.py:641
  11.0 28.8 %collective-permute-start.8 = (bf16[512,1024]{1,0:T(8,128)(2,1)S(1)}, bf16[512,1024]{1,0:T(8,128)(2,1)}, u32[]{:S(2)}, u32[]{:S(2)}) collective-permute-start(bf16[512,1024]{1,0:T(8,128)(2,1)S(1)} %norm_one.1), channel_id=1, source_target_pairs={{0,2},{1,3},{2,0},{3,1},{4,6},{5,7},{6,4},{7,5},{8,10},{9,11},{10,... | collective-permute-start | bytes 3145736 | tf_op jit(solution)/shard_map/ppermute | solution.py:524
  15.4 14.7 %collective-permute-start.1 = (bf16[128,1024]{0,1:T(8,128)(2,1)}, bf16[128,1024]{0,1:T(8,128)(2,1)}, u32[]{:S(2)}, u32[]{:S(2)}) collective-permute-start(bf16[128,1024]{0,1:T(8,128)(2,1)} %get-tuple-element.252), channel_id=1, source_target_pairs={{0,16},{4,20},{8,24},{12,28},{16,0},{20,4},{24,8},{28,12},{1,17},{... | collective-permute-start | bytes 786440 | tf_op jit(solution)/shard_map/ppermute | solution.py:524
  18.0 15.6 %collective-permute-start.3 = (bf16[128,1024]{0,1:T(8,128)(2,1)}, bf16[128,1024]{0,1:T(8,128)(2,1)}, u32[]{:S(2)}, u32[]{:S(2)}) collective-permute-start(bf16[128,1024]{0,1:T(8,128)(2,1)} %get-tuple-element.252), channel_id=1, source_target_pairs={{0,8},{4,12},{8,0},{12,4},{16,24},{20,28},{24,16},{28,20},{1,9},{5... | collective-permute-start | bytes 786440 | tf_op jit(solution)/shard_map/ppermute | solution.py:524
  30.1 7.4 %collective-permute-start.5 = (bf16[128,1024]{0,1:T(8,128)(2,1)}, bf16[128,1024]{0,1:T(8,128)(2,1)}, u32[]{:S(2)}, u32[]{:S(2)}) collective-permute-start(bf16[128,1024]{0,1:T(8,128)(2,1)} %collective-permute-done.1), channel_id=1, source_target_pairs={{0,8},{4,12},{8,0},{12,4},{16,24},{20,28},{24,16},{28,20},{1,9},{5... | collective-permute-start | bytes 786440 | tf_op jit(solution)/shard_map/ppermute | solution.py:524
  37.5 327.6 %reduce-scatter.2.cloned.1.call-start = ((), (), s32[]{:S(2)}) async-start(), calls=%async_computation.2 | async-start | bytes 4718592 | tf_op jit(solution)/shard_map/reduce_scatter | solution.py:729
  37.6 32.2 %collective-permute-start.7 = (bf16[512,1024]{1,0:T(8,128)(2,1)S(1)}, bf16[512,1024]{1,0:T(8,128)(2,1)}, u32[]{:S(2)}, u32[]{:S(2)}) collective-permute-start(bf16[512,1024]{1,0:T(8,128)(2,1)S(1)} %norm_one.1), channel_id=1, source_target_pairs={{0,1},{1,0},{2,3},{3,2},{4,5},{5,4},{6,7},{7,6},{8,9},{9,8},{10,11... | collective-permute-start | bytes 3145736 | tf_op jit(solution)/shard_map/ppermute | solution.py:524
  37.7 9.4 %collective-permute-start = (bf16[128,1024]{0,1:T(8,128)(2,1)}, bf16[128,1024]{0,1:T(8,128)(2,1)S(1)}, u32[]{:S(2)}, u32[]{:S(2)}) collective-permute-start(bf16[128,1024]{0,1:T(8,128)(2,1)} %get-tuple-element.252), channel_id=1, source_target_pairs={{0,4},{4,0},{8,12},{12,8},{16,20},{20,16},{24,28},{28,24},{1,5},{5... | collective-permute-start | bytes 786440 | tf_op jit(solution)/shard_map/ppermute | solution.py:524
  39.2 33.0 %collective-permute-start.10 = (bf16[512,1024]{1,0:T(8,128)(2,1)}, bf16[512,1024]{1,0:T(8,128)(2,1)}, u32[]{:S(2)}, u32[]{:S(2)}) collective-permute-start(bf16[512,1024]{1,0:T(8,128)(2,1)} %refs_9_.1), channel_id=1, source_target_pairs={{0,2},{1,3},{2,0},{3,1},{4,6},{5,7},{6,4},{7,5},{8,10},{9,11},{10,... | collective-permute-start | bytes 3145736 | tf_op jit(solution)/shard_map/ppermute | solution.py:524
  39.7 30.0 %collective-permute-start.9 = (bf16[512,1024]{1,0:T(8,128)(2,1)}, bf16[512,1024]{1,0:T(8,128)(2,1)}, u32[]{:S(2)}, u32[]{:S(2)}) collective-permute-start(bf16[512,1024]{1,0:T(8,128)(2,1)} %collective-permute-done.8), channel_id=1, source_target_pairs={{0,1},{1,0},{2,3},{3,2},{4,5},{5,4},{6,7},{7,6},{8,9},{9,8},{10,11... | collective-permute-start | bytes 3145736 | tf_op jit(solution)/shard_map/ppermute | solution.py:524
  39.8 16.1 %collective-permute-start.2 = (bf16[128,1024]{0,1:T(8,128)(2,1)}, bf16[128,1024]{0,1:T(8,128)(2,1)}, u32[]{:S(2)}, u32[]{:S(2)}) collective-permute-start(bf16[128,1024]{0,1:T(8,128)(2,1)} %collective-permute-done.1), channel_id=1, source_target_pairs={{0,4},{4,0},{8,12},{12,8},{16,20},{20,16},{24,28},{28,24},{1,5},{5... | collective-permute-start | bytes 786440 | tf_op jit(solution)/shard_map/ppermute | solution.py:524
  47.0 16.9 %collective-permute-start.4 = (bf16[128,1024]{0,1:T(8,128)(2,1)}, bf16[128,1024]{0,1:T(8,128)(2,1)S(1)}, u32[]{:S(2)}, u32[]{:S(2)}) collective-permute-start(bf16[128,1024]{0,1:T(8,128)(2,1)} %collective-permute-done.3), channel_id=1, source_target_pairs={{0,4},{4,0},{8,12},{12,8},{16,20},{20,16},{24,28},{28,24},{1,5},{5... | collective-permute-start | bytes 786440 | tf_op jit(solution)/shard_map/ppermute | solution.py:524
  55.8 13.2 %collective-permute-start.6 = (bf16[128,1024]{0,1:T(8,128)(2,1)}, bf16[128,1024]{0,1:T(8,128)(2,1)S(1)}, u32[]{:S(2)}, u32[]{:S(2)}) collective-permute-start(bf16[128,1024]{0,1:T(8,128)(2,1)} %collective-permute-done.5), channel_id=1, source_target_pairs={{0,4},{4,0},{8,12},{12,8},{16,20},{20,16},{24,28},{28,24},{1,5},{5... | collective-permute-start | bytes 786440 | tf_op jit(solution)/shard_map/ppermute | solution.py:524
  69.2 21.0 %collective-permute-start.11 = (bf16[1024,256]{0,1:T(8,128)(2,1)S(1)}, bf16[1024,256]{0,1:T(8,128)(2,1)S(1)}, u32[]{:S(2)}, u32[]{:S(2)}) collective-permute-start(bf16[1024,256]{0,1:T(8,128)(2,1)S(1)} %slice.331), channel_id=1, source_target_pairs={{0,2},{1,3},{2,0},{3,1},{4,6},{5,7},{6,4},{7,5},{8,10},{9,11},{10,... | collective-permute-start | bytes 1572872 | tf_op jit(solution)/shard_map/ppermute | solution.py:524
  90.3 15.9 %collective-permute-start.12 = (bf16[128,512]{1,0:T(8,128)(2,1)S(1)}, bf16[128,512]{1,0:T(8,128)(2,1)S(1)}, u32[]{:S(2)}, u32[]{:S(2)}) collective-permute-start(bf16[128,512]{1,0:T(8,128)(2,1)S(1)} %get-tuple-element.249), channel_id=1, source_target_pairs={{0,1},{1,0},{2,3},{3,2},{4,5},{5,4},{6,7},{7,6},{8,9},{9,8},{10,11... | collective-permute-start | bytes 393224 | tf_op jit(solution)/shard_map/ppermute | solution.py:524
  90.4 15.9 %collective-permute-start.13 = (bf16[128,512]{1,0:T(8,128)(2,1)S(1)}, bf16[128,512]{1,0:T(8,128)(2,1)S(1)}, u32[]{:S(2)}, u32[]{:S(2)}) collective-permute-start(bf16[128,512]{1,0:T(8,128)(2,1)S(1)} %get-tuple-element.248), channel_id=1, source_target_pairs={{0,2},{1,3},{2,0},{3,1},{4,6},{5,7},{6,4},{7,5},{8,10},{9,11},{10,... | collective-permute-start | bytes 393224 | tf_op jit(solution)/shard_map/ppermute | solution.py:524
  91.9 14.4 %collective-permute-start.14 = (bf16[128,512]{1,0:T(8,128)(2,1)S(1)}, bf16[128,512]{1,0:T(8,128)(2,1)S(1)}, u32[]{:S(2)}, u32[]{:S(2)}) collective-permute-start(bf16[128,512]{1,0:T(8,128)(2,1)S(1)} %get-tuple-element.247), channel_id=1, source_target_pairs={{0,3},{1,2},{2,1},{3,0},{4,7},{5,6},{6,5},{7,4},{8,11},{9,10},{10,... | collective-permute-start | bytes 393224 | tf_op jit(solution)/shard_map/ppermute | solution.py:524
  106.3 2.6 collective-permute-start.15
  107.0 16.9 %collective-permute-start.22 = (bf16[512,1024]{1,0:T(8,128)(2,1)}, bf16[512,1024]{1,0:T(8,128)(2,1)}, u32[]{:S(2)}, u32[]{:S(2)}) collective-permute-start(bf16[512,1024]{1,0:T(8,128)(2,1)} %refs_9_.1), channel_id=1, source_target_pairs={{0,1},{1,0},{2,3},{3,2},{4,5},{5,4},{6,7},{7,6},{8,9},{9,8},{10,11... | collective-permute-start | bytes 3145736 | tf_op jit(solution)/shard_map/ppermute | solution.py:524
  107.0 8.8 %collective-permute-start.18 = (bf16[1024,256]{0,1:T(8,128)(2,1)S(1)}, bf16[1024,256]{0,1:T(8,128)(2,1)S(1)}, u32[]{:S(2)}, u32[]{:S(2)}) collective-permute-start(bf16[1024,256]{0,1:T(8,128)(2,1)S(1)} %slice.331), channel_id=1, source_target_pairs={{0,1},{1,0},{2,3},{3,2},{4,5},{5,4},{6,7},{7,6},{8,9},{9,8},{10,11... | collective-permute-start | bytes 1572872 | tf_op jit(solution)/shard_map/ppermute | solution.py:524
  107.5 8.4 %collective-permute-start.19 = (bf16[1024,256]{0,1:T(8,128)(2,1)S(1)}, bf16[1024,256]{0,1:T(8,128)(2,1)S(1)}, u32[]{:S(2)}, u32[]{:S(2)}) collective-permute-start(bf16[1024,256]{0,1:T(8,128)(2,1)S(1)} %collective-permute-done.11), channel_id=1, source_target_pairs={{0,1},{1,0},{2,3},{3,2},{4,5},{5,4},{6,7},{7,6},{8,9},{9,8},{10,11... | collective-permute-start | bytes 1572872 | tf_op jit(solution)/shard_map/ppermute | solution.py:524
  107.5 6.3 %collective-permute-start.16 = (bf16[128,512]{1,0:T(8,128)(2,1)S(1)}, bf16[128,512]{1,0:T(8,128)(2,1)S(1)}, u32[]{:S(2)}, u32[]{:S(2)}) collective-permute-start(bf16[128,512]{1,0:T(8,128)(2,1)S(1)} %get-tuple-element.244), channel_id=1, source_target_pairs={{0,2},{1,3},{2,0},{3,1},{4,6},{5,7},{6,4},{7,5},{8,10},{9,11},{10,... | collective-permute-start | bytes 393224 | tf_op jit(solution)/shard_map/ppermute | solution.py:524
  108.9 6.8 %collective-permute-start.17 = (bf16[128,512]{1,0:T(8,128)(2,1)S(1)}, bf16[128,512]{1,0:T(8,128)(2,1)S(1)}, u32[]{:S(2)}, u32[]{:S(2)}) collective-permute-start(bf16[128,512]{1,0:T(8,128)(2,1)S(1)} %get-tuple-element.243), channel_id=1, source_target_pairs={{0,3},{1,2},{2,1},{3,0},{4,7},{5,6},{6,5},{7,4},{8,11},{9,10},{10,... | collective-permute-start | bytes 393224 | tf_op jit(solution)/shard_map/ppermute | solution.py:524
  121.4 2.4 collective-permute-start.20
  122.2 2.0 collective-permute-start.21
  122.5 24.2 %collective-permute-start.27 = (bf16[512,1024]{1,0:T(8,128)(2,1)}, bf16[512,1024]{1,0:T(8,128)(2,1)}, u32[]{:S(2)}, u32[]{:S(2)}) collective-permute-start(bf16[512,1024]{1,0:T(8,128)(2,1)} %collective-permute-done.10.refs_2_.refs_12_.refs_14_), channel_id=1, source_target_pairs={{0,1},{1,0},{2,3},{3,2},{4,5},{5,4},{6,7},{7,6},{8,9},{9,8},{10,11... | collective-permute-start | bytes 3145736 | tf_op jit(solution)/shard_map/ppermute | solution.py:524
  122.7 22.5 %collective-permute-start.25 = (bf16[256,1024]{1,0:T(8,128)(2,1)}, bf16[256,1024]{1,0:T(8,128)(2,1)}, u32[]{:S(2)}, u32[]{:S(2)}) collective-permute-start(bf16[256,1024]{1,0:T(8,128)(2,1)} %get-tuple-element.105.refs_0_), channel_id=1, source_target_pairs={{0,2},{1,3},{2,0},{3,1},{4,6},{5,7},{6,4},{7,5},{8,10},{9,11},{10,... | collective-permute-start | bytes 1572872 | tf_op jit(solution)/shard_map/ppermute | solution.py:524
  145.2 2.1 collective-permute-start.26
  145.4 14.1 %collective-permute-start.30 = (bf16[256,1024]{1,0:T(8,128)(2,1)S(1)}, bf16[256,1024]{1,0:T(8,128)(2,1)S(1)}, u32[]{:S(2)}, u32[]{:S(2)}) collective-permute-start(bf16[256,1024]{1,0:T(8,128)(2,1)S(1)} %copy-done.36), channel_id=1, source_target_pairs={{0,2},{1,3},{2,0},{3,1},{4,6},{5,7},{6,4},{7,5},{8,10},{9,11},{10,... | collective-permute-start | bytes 1572872 | tf_op jit(solution)/shard_map/ppermute | solution.py:524
  157.1 2.4 collective-permute-start.28
  159.5 1.9 collective-permute-start.31
  159.7 14.4 %collective-permute-start.29 = (bf16[256,1024]{1,0:T(8,128)(2,1)S(1)}, bf16[256,1024]{1,0:T(8,128)(2,1)S(1)}, u32[]{:S(2)}, u32[]{:S(2)}) collective-permute-start(bf16[256,1024]{1,0:T(8,128)(2,1)S(1)} %add_convert_fusion.9), channel_id=1, source_target_pairs={{0,2},{1,3},{2,0},{3,1},{4,6},{5,7},{6,4},{7,5},{8,10},{9,11},{10,... | collective-permute-start | bytes 1572872 | tf_op jit(solution)/shard_map/ppermute | solution.py:524
  174.9 2.6 collective-permute-start.32
  174.9 19.7 %collective-permute-start.23 = (bf16[256,1024]{1,0:T(8,128)(2,1)}, bf16[256,1024]{1,0:T(8,128)(2,1)}, u32[]{:S(2)}, u32[]{:S(2)}) collective-permute-start(bf16[256,1024]{1,0:T(8,128)(2,1)} %get-tuple-element.114), channel_id=1, source_target_pairs={{0,1},{1,0},{2,3},{3,2},{4,5},{5,4},{6,7},{7,6},{8,9},{9,8},{10,11... | collective-permute-start | bytes 1572872 | tf_op jit(solution)/shard_map/ppermute | solution.py:524
  175.5 19.2 %collective-permute-start.24 = (bf16[256,1024]{1,0:T(8,128)(2,1)}, bf16[256,1024]{1,0:T(8,128)(2,1)}, u32[]{:S(2)}, u32[]{:S(2)}) collective-permute-start(bf16[256,1024]{1,0:T(8,128)(2,1)} %get-tuple-element.115), channel_id=1, source_target_pairs={{0,1},{1,0},{2,3},{3,2},{4,5},{5,4},{6,7},{7,6},{8,9},{9,8},{10,11... | collective-permute-start | bytes 1572872 | tf_op jit(solution)/shard_map/ppermute | solution.py:524
  178.6 16.0 %collective-permute-start.33 = (bf16[256,1024]{1,0:T(8,128)(2,1)}, bf16[256,1024]{1,0:T(8,128)(2,1)}, u32[]{:S(2)}, u32[]{:S(2)}) collective-permute-start(bf16[256,1024]{1,0:T(8,128)(2,1)} %add_convert_fusion.8), channel_id=1, source_target_pairs={{0,2},{1,3},{2,0},{3,1},{4,6},{5,7},{6,4},{7,5},{8,10},{9,11},{10,... | collective-permute-start | bytes 1572872 | tf_op jit(solution)/shard_map/ppermute | solution.py:524
  204.8 19.5 %collective-permute-start.36 = (bf16[256,1024]{1,0:T(8,128)(2,1)S(1)}, bf16[256,1024]{1,0:T(8,128)(2,1)S(1)}, u32[]{:S(2)}, u32[]{:S(2)}) collective-permute-start(bf16[256,1024]{1,0:T(8,128)(2,1)S(1)} %copy-done.34), channel_id=1, source_target_pairs={{0,1},{1,0},{2,3},{3,2},{4,5},{5,4},{6,7},{7,6},{8,9},{9,8},{10,11... | collective-permute-start | bytes 1572872 | tf_op jit(solution)/shard_map/ppermute | solution.py:524
  207.3 15.0 %collective-permute-start.37 = (bf16[1024,256]{0,1:T(8,128)(2,1)S(1)}, bf16[1024,256]{0,1:T(8,128)(2,1)S(1)}, u32[]{:S(2)}, u32[]{:S(2)}) collective-permute-start(bf16[1024,256]{0,1:T(8,128)(2,1)S(1)} %get-tuple-element.209), channel_id=1, source_target_pairs={{0,1},{1,0},{2,3},{3,2},{4,5},{5,4},{6,7},{7,6},{8,9},{9,8},{10,11... | collective-permute-start | bytes 1572872 | tf_op jit(solution)/shard_map/ppermute | solution.py:524
  207.5 5.3 %collective-permute-start.45 = (bf16[128,512]{1,0:T(8,128)(2,1)S(1)}, bf16[128,512]{1,0:T(8,128)(2,1)S(1)}, u32[]{:S(2)}, u32[]{:S(2)}) collective-permute-start(bf16[128,512]{1,0:T(8,128)(2,1)S(1)} %get-tuple-element.222), channel_id=1, source_target_pairs={{0,3},{1,2},{2,1},{3,0},{4,7},{5,6},{6,5},{7,4},{8,11},{9,10},{10,... | collective-permute-start | bytes 393224 | tf_op jit(solution)/shard_map/ppermute | solution.py:524
  208.5 7.6 %collective-permute-start.44 = (bf16[128,512]{1,0:T(8,128)(2,1)S(1)}, bf16[128,512]{1,0:T(8,128)(2,1)S(1)}, u32[]{:S(2)}, u32[]{:S(2)}) collective-permute-start(bf16[128,512]{1,0:T(8,128)(2,1)S(1)} %get-tuple-element.223), channel_id=1, source_target_pairs={{0,2},{1,3},{2,0},{3,1},{4,6},{5,7},{6,4},{7,5},{8,10},{9,11},{10,... | collective-permute-start | bytes 393224 | tf_op jit(solution)/shard_map/ppermute | solution.py:524
  209.5 7.9 %collective-permute-start.43 = (bf16[128,512]{1,0:T(8,128)(2,1)S(1)}, bf16[128,512]{1,0:T(8,128)(2,1)S(1)}, u32[]{:S(2)}, u32[]{:S(2)}) collective-permute-start(bf16[128,512]{1,0:T(8,128)(2,1)S(1)} %get-tuple-element.224), channel_id=1, source_target_pairs={{0,1},{1,0},{2,3},{3,2},{4,5},{5,4},{6,7},{7,6},{8,9},{9,8},{10,11... | collective-permute-start | bytes 393224 | tf_op jit(solution)/shard_map/ppermute | solution.py:524
  212.8 5.2 %collective-permute-start.42 = (bf16[128,512]{1,0:T(8,128)(2,1)S(1)}, bf16[128,512]{1,0:T(8,128)(2,1)S(1)}, u32[]{:S(2)}, u32[]{:S(2)}) collective-permute-start(bf16[128,512]{1,0:T(8,128)(2,1)S(1)} %get-tuple-element.226), channel_id=1, source_target_pairs={{0,3},{1,2},{2,1},{3,0},{4,7},{5,6},{6,5},{7,4},{8,11},{9,10},{10,... | collective-permute-start | bytes 393224 | tf_op jit(solution)/shard_map/ppermute | solution.py:524
  216.2 5.5 %collective-permute-start.41 = (bf16[128,512]{1,0:T(8,128)(2,1)S(1)}, bf16[128,512]{1,0:T(8,128)(2,1)S(1)}, u32[]{:S(2)}, u32[]{:S(2)}) collective-permute-start(bf16[128,512]{1,0:T(8,128)(2,1)S(1)} %get-tuple-element.227), channel_id=1, source_target_pairs={{0,2},{1,3},{2,0},{3,1},{4,6},{5,7},{6,4},{7,5},{8,10},{9,11},{10,... | collective-permute-start | bytes 393224 | tf_op jit(solution)/shard_map/ppermute | solution.py:524
  217.3 4.4 %collective-permute-start.40 = (bf16[128,512]{1,0:T(8,128)(2,1)S(1)}, bf16[128,512]{1,0:T(8,128)(2,1)S(1)}, u32[]{:S(2)}, u32[]{:S(2)}) collective-permute-start(bf16[128,512]{1,0:T(8,128)(2,1)S(1)} %get-tuple-element.228), channel_id=1, source_target_pairs={{0,1},{1,0},{2,3},{3,2},{4,5},{5,4},{6,7},{7,6},{8,9},{9,8},{10,11... | collective-permute-start | bytes 393224 | tf_op jit(solution)/shard_map/ppermute | solution.py:524
  218.0 6.6 %collective-permute-start.35 = (bf16[256,1024]{1,0:T(8,128)(2,1)S(1)}, bf16[256,1024]{1,0:T(8,128)(2,1)S(1)}, u32[]{:S(2)}, u32[]{:S(2)}) collective-permute-start(bf16[256,1024]{1,0:T(8,128)(2,1)S(1)} %copy-done.32), channel_id=1, source_target_pairs={{0,1},{1,0},{2,3},{3,2},{4,5},{5,4},{6,7},{7,6},{8,9},{9,8},{10,11... | collective-permute-start | bytes 1572872 | tf_op jit(solution)/shard_map/ppermute | solution.py:524
  221.7 72.3 %collective-permute-start.34 = (bf16[512,1024]{1,0:T(8,128)(2,1)}, bf16[512,1024]{1,0:T(8,128)(2,1)}, u32[]{:S(2)}, u32[]{:S(2)}) collective-permute-start(bf16[512,1024]{1,0:T(8,128)(2,1)} %pad_maximum_fusion.3), channel_id=1, source_target_pairs={{0,1},{1,0},{2,3},{3,2},{4,5},{5,4},{6,7},{7,6},{8,9},{9,8},{10,11... | collective-permute-start | bytes 3145736 | tf_op jit(solution)/shard_map/ppermute | solution.py:524
  221.7 53.7 %collective-permute-start.47 = (bf16[1024,256]{0,1:T(8,128)(2,1)}, bf16[1024,256]{0,1:T(8,128)(2,1)}, u32[]{:S(2)}, u32[]{:S(2)}) collective-permute-start(bf16[1024,256]{0,1:T(8,128)(2,1)} %get-tuple-element.208), channel_id=1, source_target_pairs={{0,1},{1,0},{2,3},{3,2},{4,5},{5,4},{6,7},{7,6},{8,9},{9,8},{10,11... | collective-permute-start | bytes 1572872 | tf_op jit(solution)/shard_map/ppermute | solution.py:524
  223.3 30.7 %collective-permute-start.38 = (bf16[1024,256]{0,1:T(8,128)(2,1)}, bf16[1024,256]{0,1:T(8,128)(2,1)}, u32[]{:S(2)}, u32[]{:S(2)}) collective-permute-start(bf16[1024,256]{0,1:T(8,128)(2,1)} %add_convert_fusion.5), channel_id=1, source_target_pairs={{0,2},{1,3},{2,0},{3,1},{4,6},{5,7},{6,4},{7,5},{8,10},{9,11},{10,... | collective-permute-start | bytes 1572872 | tf_op jit(solution)/shard_map/ppermute | solution.py:524
  251.5 25.6 %collective-permute-start.46 = (bf16[512,384]{0,1:T(8,128)(2,1)}, bf16[512,384]{0,1:T(8,128)(2,1)}, u32[]{:S(2)}, u32[]{:S(2)}) collective-permute-start(bf16[512,384]{0,1:T(8,128)(2,1)} %pad_maximum_fusion.11), channel_id=1, source_target_pairs={{0,4},{4,0},{8,12},{12,8},{16,20},{20,16},{24,28},{28,24},{1,5},{5... | collective-permute-start | bytes 1179656 | tf_op jit(solution)/shard_map/ppermute | solution.py:524
  254.0 24.8 %collective-permute-start.39 = (bf16[512,1024]{1,0:T(8,128)(2,1)}, bf16[512,1024]{1,0:T(8,128)(2,1)}, u32[]{:S(2)}, u32[]{:S(2)}) collective-permute-start(bf16[512,1024]{1,0:T(8,128)(2,1)} %pad_maximum_fusion.4), channel_id=1, source_target_pairs={{0,2},{1,3},{2,0},{3,1},{4,6},{5,7},{6,4},{7,5},{8,10},{9,11},{10,... | collective-permute-start | bytes 3145736 | tf_op jit(solution)/shard_map/ppermute | solution.py:524
  289.4 8.3 %collective-permute-start.48 = (bf16[512,1024]{1,0:T(8,128)(2,1)}, bf16[512,1024]{1,0:T(8,128)(2,1)}, u32[]{:S(2)}, u32[]{:S(2)}) collective-permute-start(bf16[512,1024]{1,0:T(8,128)(2,1)} %slice.347), channel_id=1, source_target_pairs={{0,1},{1,0},{2,3},{3,2},{4,5},{5,4},{6,7},{7,6},{8,9},{9,8},{10,11... | collective-permute-start | bytes 3145736 | tf_op jit(solution)/shard_map/ppermute | solution.py:524
  289.4 22.5 %collective-permute-start.58 = (bf16[512,640]{0,1:T(8,128)(2,1)}, bf16[512,640]{0,1:T(8,128)(2,1)}, u32[]{:S(2)}, u32[]{:S(2)}) collective-permute-start(bf16[512,640]{0,1:T(8,128)(2,1)} %pad_maximum_fusion.7), channel_id=1, source_target_pairs={{0,4},{4,0},{8,12},{12,8},{16,20},{20,16},{24,28},{28,24},{1,5},{5... | collective-permute-start | bytes 1966088 | tf_op jit(solution)/shard_map/ppermute | solution.py:524
  300.4 58.7 %collective-permute-start.50 = (bf16[512,1024]{1,0:T(8,128)(2,1)}, bf16[512,1024]{1,0:T(8,128)(2,1)S(1)}, u32[]{:S(2)}, u32[]{:S(2)}) collective-permute-start(bf16[512,1024]{1,0:T(8,128)(2,1)} %add_convert_fusion.2), channel_id=1, source_target_pairs={{0,2},{1,3},{2,0},{3,1},{4,6},{5,7},{6,4},{7,5},{8,10},{9,11},{10,... | collective-permute-start | bytes 3145736 | tf_op jit(solution)/shard_map/ppermute | solution.py:524
  303.0 11.7 %collective-permute-start.52 = (f32[60,128]{1,0:T(8,128)S(1)}, f32[60,128]{1,0:T(8,128)S(1)}, u32[]{:S(2)}, u32[]{:S(2)}) collective-permute-start(f32[60,128]{1,0:T(8,128)S(1)} %pad_maximum_fusion.18), channel_id=1, source_target_pairs={{0,8},{4,12},{8,0},{12,4},{16,24},{20,28},{24,16},{28,20},{1,9},{5... | collective-permute-start | bytes 92168 | tf_op jit(solution)/shard_map/ppermute | solution.py:524
  304.7 9.9 %collective-permute-start.53 = (f32[60,128]{1,0:T(8,128)S(1)}, f32[60,128]{1,0:T(8,128)S(1)}, u32[]{:S(2)}, u32[]{:S(2)}) collective-permute-start(f32[60,128]{1,0:T(8,128)S(1)} %pad_maximum_fusion.18), channel_id=1, source_target_pairs={{0,12},{4,8},{8,4},{12,0},{16,28},{20,24},{24,20},{28,16},{1,13},{... | collective-permute-start | bytes 92168 | tf_op jit(solution)/shard_map/ppermute | solution.py:524
  306.0 8.7 %collective-permute-start.51 = (f32[60,128]{1,0:T(8,128)S(1)}, f32[60,128]{1,0:T(8,128)S(1)}, u32[]{:S(2)}, u32[]{:S(2)}) collective-permute-start(f32[60,128]{1,0:T(8,128)S(1)} %pad_maximum_fusion.18), channel_id=1, source_target_pairs={{0,4},{4,0},{8,12},{12,8},{16,20},{20,16},{24,28},{28,24},{1,5},{5... | collective-permute-start | bytes 92168 | tf_op jit(solution)/shard_map/ppermute | solution.py:524
  311.9 47.2 %collective-permute-start.49 = (bf16[512,1024]{1,0:T(8,128)(2,1)}, bf16[512,1024]{1,0:T(8,128)(2,1)}, u32[]{:S(2)}, u32[]{:S(2)}) collective-permute-start(bf16[512,1024]{1,0:T(8,128)(2,1)} %get-tuple-element.206), channel_id=1, source_target_pairs={{0,1},{1,0},{2,3},{3,2},{4,5},{5,4},{6,7},{7,6},{8,9},{9,8},{10,11... | collective-permute-start | bytes 3145736 | tf_op jit(solution)/shard_map/ppermute | solution.py:524
  314.7 5.4 %collective-permute-start.54 = (f32[60,128]{1,0:T(8,128)S(1)}, f32[60,128]{1,0:T(8,128)S(1)}, u32[]{:S(2)}, u32[]{:S(2)}) collective-permute-start(f32[60,128]{1,0:T(8,128)S(1)} %add_add_fusion.1), channel_id=1, source_target_pairs={{0,16},{4,20},{8,24},{12,28},{16,0},{20,4},{24,8},{28,12},{1,17},{... | collective-permute-start | bytes 92168 | tf_op jit(solution)/shard_map/ppermute | solution.py:524
  320.1 6.6 %collective-permute-start.56 = (f32[48,128]{1,0:T(8,128)S(1)}, f32[48,128]{1,0:T(8,128)S(1)}, u32[]{:S(2)}, u32[]{:S(2)}) collective-permute-start(f32[48,128]{1,0:T(8,128)S(1)} %slice.358), channel_id=1, source_target_pairs={{0,2},{1,3},{2,0},{3,1},{4,6},{5,7},{6,4},{7,5},{8,10},{9,11},{10,... | collective-permute-start | bytes 73736 | tf_op jit(solution)/shard_map/ppermute | solution.py:524
  321.1 10.0 %collective-permute-start.57 = (f32[48,128]{1,0:T(8,128)S(1)}, f32[48,128]{1,0:T(8,128)S(1)}, u32[]{:S(2)}, u32[]{:S(2)}) collective-permute-start(f32[48,128]{1,0:T(8,128)S(1)} %slice.358), channel_id=1, source_target_pairs={{0,3},{1,2},{2,1},{3,0},{4,7},{5,6},{6,5},{7,4},{8,11},{9,10},{10,... | collective-permute-start | bytes 73736 | tf_op jit(solution)/shard_map/ppermute | solution.py:524
  321.4 9.6 %collective-permute-start.55 = (f32[48,128]{1,0:T(8,128)S(1)}, f32[48,128]{1,0:T(8,128)}, u32[]{:S(2)}, u32[]{:S(2)}) collective-permute-start(f32[48,128]{1,0:T(8,128)S(1)} %slice.358), channel_id=1, source_target_pairs={{0,1},{1,0},{2,3},{3,2},{4,5},{5,4},{6,7},{7,6},{8,9},{9,8},{10,11... | collective-permute-start | bytes 73736 | tf_op jit(solution)/shard_map/ppermute | solution.py:524
  326.7 12.0 %collective-permute-start.61 = (bf16[128,1024]{0,1:T(8,128)(2,1)}, bf16[128,1024]{0,1:T(8,128)(2,1)}, u32[]{:S(2)}, u32[]{:S(2)}) collective-permute-start(bf16[128,1024]{0,1:T(8,128)(2,1)} %get-tuple-element.219), channel_id=1, source_target_pairs={{0,24},{4,28},{8,16},{12,20},{16,8},{20,12},{24,0},{28,4},{1,25},{... | collective-permute-start | bytes 786440 | tf_op jit(solution)/shard_map/ppermute | solution.py:524
  331.0 21.6 %collective-permute-start.60 = (bf16[128,1024]{0,1:T(8,128)(2,1)}, bf16[128,1024]{0,1:T(8,128)(2,1)}, u32[]{:S(2)}, u32[]{:S(2)}) collective-permute-start(bf16[128,1024]{0,1:T(8,128)(2,1)} %get-tuple-element.220), channel_id=1, source_target_pairs={{0,16},{4,20},{8,24},{12,28},{16,0},{20,4},{24,8},{28,12},{1,17},{... | collective-permute-start | bytes 786440 | tf_op jit(solution)/shard_map/ppermute | solution.py:524
  331.0 21.6 %collective-permute-start.59 = (bf16[128,1024]{0,1:T(8,128)(2,1)S(1)}, bf16[128,1024]{0,1:T(8,128)(2,1)}, u32[]{:S(2)}, u32[]{:S(2)}) collective-permute-start(bf16[128,1024]{0,1:T(8,128)(2,1)S(1)} %get-tuple-element.218), channel_id=1, source_target_pairs={{0,8},{4,12},{8,0},{12,4},{16,24},{20,28},{24,16},{28,20},{1,9},{5... | collective-permute-start | bytes 786440 | tf_op jit(solution)/shard_map/ppermute | solution.py:524
  (96 other events, 465.1 us)
Sparse Core Ops, SparseCore 0:
  37.7 77.7 all-gather.1
  194.7 89.5 reduce-scatter.1
